TPU v7x, 32 devices: a whole 2x2x4 slice. The times are simulated.
32 devices in a mesh: tower: 2 (over y), dp: 4 (over z), fsdp: 4 (over x, core).
Axes of the slice: x: 2, y: 2, z: 4, core: 2. Of those that a mesh axis runs over, the one named last changes fastest.
Arguments:
- tokens_in: bfloat16 [2, 2, 16, 512, 768], P('tower', None, ('dp', 'fsdp')), may hold values from -6 to 6
- query_lengths: int32 [2, 16, 8], P(None, ('dp', 'fsdp')), may hold values from 1 to 256, 512 in all within a row
- positive_ids: int32 [2, 16, 8], P(None, ('dp', 'fsdp')), may hold values from 0 to 15
- gain_attn: float32 [768], P('fsdp'), may hold values from 0.1 to 1.9
- gain_ffn: float32 [768], P('fsdp'), may hold values from 0.1 to 1.9
- w_query: float32 [768, 768], P('fsdp'), may hold values from -0.09375 to 0.09375
- w_key: float32 [768, 768], P('fsdp'), may hold values from -0.09375 to 0.09375
- w_value: float32 [768, 768], P('fsdp'), may hold values from -0.21875 to 0.21875
- w_out: float32 [768, 768], P('fsdp'), may hold values from -1.75 to 1.75
- rel_bias: float32 [32, 12], P('fsdp'), may hold values from -4 to 4
- w_in: float32 [768, 3072], P('fsdp'), may hold values from -0.21875 to 0.21875
- w_ffn_out: float32 [3072, 768], P('fsdp'), may hold values from -0.109375 to 0.109375
- w_proj: float32 [768, 768], P('fsdp'), may hold values from -0.21875 to 0.21875
Outputs:
- query_loss: float32 [2, 16, 8], P(None, ('dp', 'fsdp'))
- grad_tokens: bfloat16 [2, 2, 16, 512, 768], P('tower', None, ('dp', 'fsdp'))
- grad_gain_attn: float32 [768], P('fsdp')
- grad_gain_ffn: float32 [768], P('fsdp')
- grad_w_query: float32 [768, 768], P('fsdp')
- grad_w_key: float32 [768, 768], P('fsdp')
- grad_w_value: float32 [768, 768], P('fsdp')
- grad_w_out: float32 [768, 768], P('fsdp')
- grad_rel_bias: float32 [32, 12], P('fsdp')
- grad_w_in: float32 [768, 3072], P('fsdp')
- grad_w_ffn_out: float32 [3072, 768], P('fsdp')
- grad_w_proj: float32 [768, 768], P('fsdp')
Inputs may be any that keep to these rules, and one draw needn't show every extreme that they name: `query_lengths`: in every row the 8 lengths sum to 512, and the longest is exactly 256.
All inputs are finite; a program needn't handle non-finite values.
Results may differ from a plain program's by a relative error of at most 0.018.
The roundings to bfloat16 on the way count: a program that leaves them out, or rounds other values in their place, can miss the bound.
Values may be sent and summed in bfloat16 or wider, within the bound.
No kernel may reach another device: no remote copies, remote signals or barrier semaphores. Data moves between devices by JAX's collectives and lax.ppermute only.
A program may use at most 192 MiB of HBM per device.

v0:
```python
import jax
import jax.numpy as jnp
from jax import lax
from jax.sharding import PartitionSpec as P

D = 768
H = 12
DH = 64
P_SIZE = 768
NB = 32
SEQ = 512
PLEN = 512
QSEG = 8
MB = 2
PSEG = 1


EPSILON = 1e-06
LOGIT_SCALE = 50.0
LOSS_SCALE = 256.0
THRESHOLDS = (12, 16, 23, 32, 46, 64, 91)
MASKED = -1e30
HIGHEST = lax.Precision.HIGHEST


def from_behind(block, axis, distance):
    devices = range(lax.axis_size(axis))
    route = [(i - distance, i) for i in devices if i - distance in devices]
    return lax.ppermute(block, axis, route)


def bucket_rows(block_rows, width):
    query_place = lax.broadcasted_iota(jnp.int32, (block_rows, width), 0)
    key_place = lax.broadcasted_iota(jnp.int32, (block_rows, width), 1)
    offset = key_place - query_place
    distance = jnp.abs(offset)
    far_bucket = 8 + sum(((distance >= threshold).astype(jnp.int32) for threshold in THRESHOLDS))
    inside = jnp.where(distance < 8, distance, far_bucket)
    return jnp.where(offset > 0, 16, 0) + inside


def segments_of(lengths, is_query):
    row_count = lengths.shape[0]
    ends_at = jnp.cumsum(lengths, axis=-1)
    places = lax.broadcasted_iota(jnp.int32, (row_count, SEQ, QSEG), 1)
    query_segment = jnp.sum((places >= ends_at[:, None, :]).astype(jnp.int32), axis=-1)
    passage_segment = lax.broadcasted_iota(jnp.int32, (row_count, SEQ), 1) // PLEN
    slot_ids = lax.broadcasted_iota(jnp.int32, lengths.shape, 1)
    passage_count = jnp.where(slot_ids < PSEG, PLEN, 0)
    return (
        jnp.where(is_query, query_segment, passage_segment),
        jnp.where(is_query, lengths, passage_count),
    )


def norm_forward(values_in, gain_vec):
    inverse = lax.rsqrt(jnp.mean(values_in * values_in, axis=-1, keepdims=True) + EPSILON)
    scaled = values_in * inverse
    return (inverse, scaled, (scaled * gain_vec).astype(jnp.bfloat16))


def norm_backward(grad_normed, inverse, scaled, gain_vec):
    grad_scaled = grad_normed * gain_vec
    grad_input = inverse * (
        grad_scaled - scaled * jnp.mean(grad_scaled * scaled, axis=-1, keepdims=True)
    )
    return (grad_input, jnp.sum(grad_normed * scaled, axis=0))


def block_scores(block_queries, row_keys, bias_block, row_segment, row_start, block_rows):
    scores = (
        jnp.einsum("ihd,jhd->hij", block_queries, row_keys, preferred_element_type=jnp.float32)
        + bias_block
    )
    same_segment = row_segment[row_start : row_start + block_rows, None] == row_segment[None, :]
    return jnp.where(same_segment[None], scores, MASKED)


def attend_rows(queries, keys_all, values_all, segment, bias_blocks):
    block_rows = min(512, SEQ)

    def one_row(operands):
        row_queries, row_keys, row_values, row_segment = operands
        scores = block_scores(row_queries, row_keys, bias_blocks[0], row_segment, 0, block_rows)
        row_top = jnp.max(scores, axis=-1, keepdims=True)
        exponent = jnp.exp(scores - row_top)
        row_total = jnp.sum(exponent, axis=-1, keepdims=True)
        weights = (exponent / row_total).astype(jnp.bfloat16)
        head_mix = jnp.einsum(
            "hij,jhd->ihd", weights, row_values, preferred_element_type=jnp.float32
        )
        outputs = [head_mix.astype(jnp.bfloat16).reshape(block_rows, H * DH)]
        totals = [row_top[:, :, 0] + jnp.log(row_total[:, :, 0])]
        return (jnp.concatenate(outputs, axis=0), jnp.concatenate(totals, axis=1))

    return lax.map(one_row, (queries, keys_all, values_all, segment))


def attend_back(
    queries, keys_all, values_all, segment, log_totals, grad_mixed, bias_blocks, one_hots
):
    block_rows = min(512, SEQ)

    def one_row(operands):
        row_queries, row_keys, row_values, row_segment, row_totals, row_grad = operands
        grad_keys = jnp.zeros((SEQ, H, DH), jnp.float32)
        grad_values = jnp.zeros((SEQ, H, DH), jnp.float32)
        grad_table = jnp.zeros((NB, H), jnp.float32)
        scores = block_scores(row_queries, row_keys, bias_blocks[0], row_segment, 0, block_rows)
        probs = jnp.exp(scores - row_totals[:, 0:block_rows, None])
        weights = probs.astype(jnp.bfloat16)
        grad_weights = jnp.einsum(
            "ihd,jhd->hij", row_grad, row_values, preferred_element_type=jnp.float32
        )
        inner = jnp.sum(probs * grad_weights, axis=-1, keepdims=True)
        grad_scores = (probs * (grad_weights - inner)).astype(jnp.bfloat16)
        grad_queries = [
            jnp.einsum("hij,jhd->ihd", grad_scores, row_keys, preferred_element_type=jnp.float32)
        ]
        grad_keys = grad_keys + jnp.einsum(
            "hij,ihd->jhd", grad_scores, row_queries, preferred_element_type=jnp.float32
        )
        grad_values = grad_values + jnp.einsum(
            "hij,ihd->jhd", weights, row_grad, preferred_element_type=jnp.float32
        )
        grad_table = grad_table + jnp.einsum(
            "hij,ijb->bh", grad_scores, one_hots[0], preferred_element_type=jnp.float32
        )
        return (
            jnp.concatenate(grad_queries, axis=0).astype(jnp.bfloat16).reshape(SEQ, H * DH),
            grad_keys.astype(jnp.bfloat16).reshape(SEQ, H * DH),
            grad_values.astype(jnp.bfloat16).reshape(SEQ, H * DH),
            grad_table,
        )

    return lax.map(one_row, (queries, keys_all, values_all, segment, log_totals, grad_mixed))


def reduce_now(gradients):
    shards = (
        lax.psum_scatter(
            gradients[0].astype(jnp.bfloat16), "fsdp", scatter_dimension=0, tiled=True
        ).astype(jnp.float32),
        lax.psum_scatter(
            gradients[1].astype(jnp.bfloat16), "fsdp", scatter_dimension=0, tiled=True
        ).astype(jnp.float32),
        lax.psum_scatter(
            gradients[2].astype(jnp.bfloat16), "fsdp", scatter_dimension=0, tiled=True
        ).astype(jnp.float32),
        lax.psum_scatter(
            gradients[3].astype(jnp.bfloat16), "fsdp", scatter_dimension=0, tiled=True
        ).astype(jnp.float32),
        lax.psum_scatter(
            gradients[4].astype(jnp.bfloat16), "fsdp", scatter_dimension=0, tiled=True
        ).astype(jnp.float32),
        lax.psum_scatter(
            gradients[5].astype(jnp.bfloat16), "fsdp", scatter_dimension=0, tiled=True
        ).astype(jnp.float32),
        lax.psum_scatter(
            gradients[6].astype(jnp.bfloat16), "fsdp", scatter_dimension=0, tiled=True
        ).astype(jnp.float32),
        lax.psum_scatter(
            gradients[7].astype(jnp.bfloat16), "fsdp", scatter_dimension=0, tiled=True
        ).astype(jnp.float32),
        lax.psum_scatter(
            gradients[8].astype(jnp.bfloat16), "fsdp", scatter_dimension=0, tiled=True
        ).astype(jnp.float32),
        lax.psum_scatter(
            gradients[9].astype(jnp.bfloat16), "fsdp", scatter_dimension=0, tiled=True
        ).astype(jnp.float32),
    )
    return lax.psum(
        (
            shards[0],
            shards[1],
            shards[2],
            shards[3],
            shards[4],
            shards[5],
            shards[6],
            shards[7],
            shards[8],
            shards[9],
        ),
        ("tower", "dp"),
    )


def local(
    tokens_in,
    query_lengths,
    positive_ids,
    gain_attn,
    gain_ffn,
    w_query,
    w_key,
    w_value,
    w_out,
    rel_bias,
    w_in,
    w_ffn_out,
    w_proj,
):
    gathered = (
        lax.all_gather(gain_attn.astype(jnp.bfloat16), "fsdp", axis=0, tiled=True),
        lax.all_gather(gain_ffn.astype(jnp.bfloat16), "fsdp", axis=0, tiled=True),
        lax.all_gather(w_query.astype(jnp.bfloat16), "fsdp", axis=0, tiled=True),
        lax.all_gather(w_key.astype(jnp.bfloat16), "fsdp", axis=0, tiled=True),
        lax.all_gather(w_value.astype(jnp.bfloat16), "fsdp", axis=0, tiled=True),
        lax.all_gather(w_out.astype(jnp.bfloat16), "fsdp", axis=0, tiled=True),
        lax.all_gather(rel_bias.astype(jnp.bfloat16), "fsdp", axis=0, tiled=True),
        lax.all_gather(w_in.astype(jnp.bfloat16), "fsdp", axis=0, tiled=True),
        lax.all_gather(w_ffn_out.astype(jnp.bfloat16), "fsdp", axis=0, tiled=True),
        lax.all_gather(w_proj.astype(jnp.bfloat16), "fsdp", axis=0, tiled=True),
    )
    gain_one = gathered[0].astype(jnp.float32)
    gain_two = gathered[1].astype(jnp.float32)
    query_mat, key_mat, value_mat, out_mat, table_mat, in_mat, ffn_mat, proj_mat = gathered[2:]
    rows_here = tokens_in.shape[2]
    tokens_here = rows_here * SEQ
    is_query = lax.axis_index("tower") == 0
    block_rows = min(512, SEQ)
    buckets = bucket_rows(block_rows, SEQ)
    table_hot = (buckets[:, :, None] == lax.broadcasted_iota(jnp.int32, (1, 1, NB), 2)).astype(
        jnp.bfloat16
    )
    one_hots = [table_hot]
    bias_blocks = [
        jnp.einsum("ijb,bh->hij", table_hot, table_mat, preferred_element_type=jnp.float32)
    ]
    running = tuple(
        (
            jnp.zeros(master.shape, jnp.float32)
            for master in (
                gain_attn,
                gain_ffn,
                w_query,
                w_key,
                w_value,
                w_out,
                rel_bias,
                w_in,
                w_ffn_out,
                w_proj,
            )
        )
    )
    shaped = (rows_here, SEQ, H, DH)
    losses_all = []
    token_grads = []
    for micro_step in range(MB):
        segment, counts = segments_of(query_lengths[micro_step], is_query)
        inputs = tokens_in[0, micro_step].astype(jnp.float32).reshape(tokens_here, D)
        inverse_one, scaled_one, normed_one = norm_forward(inputs, gain_one)
        queries = jnp.dot(normed_one, query_mat, preferred_element_type=jnp.float32).astype(
            jnp.bfloat16
        )
        keys_all = jnp.dot(normed_one, key_mat, preferred_element_type=jnp.float32).astype(
            jnp.bfloat16
        )
        values_all = jnp.dot(normed_one, value_mat, preferred_element_type=jnp.float32).astype(
            jnp.bfloat16
        )
        query_heads = queries.reshape(shaped)
        key_heads = keys_all.reshape(shaped)
        value_heads = values_all.reshape(shaped)
        attended, log_totals = attend_rows(
            query_heads, key_heads, value_heads, segment, bias_blocks
        )
        attended = attended.reshape(tokens_here, H * DH)
        after_attn = inputs + jnp.dot(attended, out_mat, preferred_element_type=jnp.float32)
        inverse_two, scaled_two, normed_two = norm_forward(after_attn, gain_two)
        hidden_pre = jnp.dot(normed_two, in_mat, preferred_element_type=jnp.float32)
        hidden, gelu_back = jax.vjp(jax.nn.gelu, hidden_pre)
        hidden = hidden.astype(jnp.bfloat16)
        after_ffn = after_attn + jnp.dot(hidden, ffn_mat, preferred_element_type=jnp.float32)
        slot_index = lax.broadcasted_iota(jnp.int32, (rows_here, QSEG, SEQ), 1)
        pool_weights = (segment[:, None, :] == slot_index).astype(jnp.float32)
        pool_weights = pool_weights / jnp.maximum(counts, 1).astype(jnp.float32)[:, :, None]
        pooled = jnp.einsum(
            "rsi,rid->rsd", pool_weights, after_ffn.reshape(rows_here, SEQ, D), precision=HIGHEST
        ).astype(jnp.bfloat16)
        projected = jnp.einsum("rsd,dp->rsp", pooled, proj_mat, preferred_element_type=jnp.float32)
        inverse_len = lax.rsqrt(jnp.sum(projected * projected, axis=-1, keepdims=True) + EPSILON)
        unit_vecs = projected * inverse_len
        embedded = unit_vecs.astype(jnp.bfloat16)
        own_queries = embedded.reshape(rows_here * QSEG, P_SIZE)
        own_passages = embedded[:, :PSEG].reshape(rows_here * PSEG, P_SIZE)
        from_passages = from_behind(own_passages, "tower", -1)
        from_queries = from_behind(own_queries, "tower", 1)
        query_embeds = jnp.where(is_query, own_queries, from_queries)
        passage_local = jnp.where(is_query, from_passages, own_passages)
        all_passages = lax.all_gather(passage_local, ("dp", "fsdp"), axis=0, tiled=True)
        logits = LOGIT_SCALE * jnp.einsum(
            "qp,np->qn", query_embeds, all_passages, preferred_element_type=jnp.float32
        )
        logit_top = jnp.max(logits, axis=-1, keepdims=True)
        log_total = logit_top[:, 0] + jnp.log(jnp.sum(jnp.exp(logits - logit_top), axis=-1))
        targets = positive_ids[micro_step].reshape(rows_here * QSEG, 1)
        target_hot = (lax.broadcasted_iota(jnp.int32, logits.shape, 1) == targets).astype(
            jnp.float32
        )
        chosen = jnp.sum(logits * target_hot, axis=-1)
        losses_all.append((log_total - chosen).reshape(rows_here, QSEG))
        grad_logits = LOSS_SCALE * (jnp.exp(logits - log_total[:, None]) - target_hot)
        grad_query_emb = LOGIT_SCALE * jnp.dot(
            grad_logits, all_passages.astype(jnp.float32), precision=HIGHEST
        )
        grad_passage_all = LOGIT_SCALE * jnp.einsum(
            "qn,qp->np", grad_logits, query_embeds.astype(jnp.float32), precision=HIGHEST
        )
        grad_passages = lax.psum_scatter(
            grad_passage_all, ("dp", "fsdp"), scatter_dimension=0, tiled=True
        )
        passage_part = jnp.pad(
            grad_passages.reshape(rows_here, PSEG, P_SIZE), ((0, 0), (0, QSEG - PSEG), (0, 0))
        )
        grad_embedded = jnp.where(
            is_query, grad_query_emb.reshape(rows_here, QSEG, P_SIZE), passage_part
        )
        grad_projected = (
            inverse_len
            * (
                grad_embedded
                - unit_vecs * jnp.sum(unit_vecs * grad_embedded, axis=-1, keepdims=True)
            )
        ).astype(jnp.bfloat16)
        grad_proj = jnp.einsum(
            "rsd,rsp->dp", pooled, grad_projected, preferred_element_type=jnp.float32
        )
        grad_pooled = jnp.einsum(
            "rsp,dp->rsd", grad_projected, proj_mat, preferred_element_type=jnp.float32
        )
        grad_after_ffn = jnp.einsum(
            "rsi,rsd->rid", pool_weights, grad_pooled, precision=HIGHEST
        ).reshape(tokens_here, D)
        grad_branch = grad_after_ffn.astype(jnp.bfloat16)
        grad_ffn_out = jnp.einsum(
            "nf,nd->fd", hidden, grad_branch, preferred_element_type=jnp.float32
        )
        grad_hidden = jnp.einsum(
            "nd,fd->nf", grad_branch, ffn_mat, preferred_element_type=jnp.float32
        )
        grad_pre = gelu_back(grad_hidden)[0].astype(jnp.bfloat16)
        grad_in = jnp.einsum("nd,nf->df", normed_two, grad_pre, preferred_element_type=jnp.float32)
        grad_normed_two = jnp.einsum(
            "nf,df->nd", grad_pre, in_mat, preferred_element_type=jnp.float32
        )
        grad_norm_two, grad_gain_two = norm_backward(
            grad_normed_two, inverse_two, scaled_two, gain_two
        )
        grad_after_attn = grad_after_ffn + grad_norm_two
        grad_attn_branch = grad_after_attn.astype(jnp.bfloat16)
        grad_out = jnp.einsum(
            "nh,nd->hd", attended, grad_attn_branch, preferred_element_type=jnp.float32
        )
        grad_attended = jnp.einsum(
            "nd,hd->nh", grad_attn_branch, out_mat, preferred_element_type=jnp.float32
        ).astype(jnp.bfloat16)
        grad_queries, grad_keys, grad_values, grad_tables = attend_back(
            query_heads,
            key_heads,
            value_heads,
            segment,
            log_totals,
            grad_attended.reshape(shaped),
            bias_blocks,
            one_hots,
        )
        grad_queries = grad_queries.reshape(tokens_here, H * DH)
        grad_keys = grad_keys.reshape(tokens_here, H * DH)
        grad_values = grad_values.reshape(tokens_here, H * DH)
        grad_query = jnp.einsum(
            "nd,nh->dh", normed_one, grad_queries, preferred_element_type=jnp.float32
        )
        grad_key = jnp.einsum(
            "nd,nh->dh", normed_one, grad_keys, preferred_element_type=jnp.float32
        )
        grad_value = jnp.einsum(
            "nd,nh->dh", normed_one, grad_values, preferred_element_type=jnp.float32
        )
        grad_normed_one = jnp.einsum(
            "nh,dh->nd", grad_queries, query_mat, preferred_element_type=jnp.float32
        )
        grad_normed_one = grad_normed_one + jnp.einsum(
            "nh,dh->nd", grad_keys, key_mat, preferred_element_type=jnp.float32
        )
        grad_normed_one = grad_normed_one + jnp.einsum(
            "nh,dh->nd", grad_values, value_mat, preferred_element_type=jnp.float32
        )
        grad_norm_one, grad_gain_one = norm_backward(
            grad_normed_one, inverse_one, scaled_one, gain_one
        )
        token_grads.append(
            (grad_after_attn + grad_norm_one).astype(jnp.bfloat16).reshape(rows_here, SEQ, D)
        )
        local_grads = (
            grad_gain_one,
            grad_gain_two,
            grad_query,
            grad_key,
            grad_value,
            grad_out,
            jnp.sum(grad_tables, axis=0),
            grad_in,
            grad_ffn_out,
            grad_proj,
        )
        reduced = reduce_now(local_grads)
        running = tuple((before + added for before, added in zip(running, reduced)))
    query_loss = jnp.stack(losses_all)
    grad_tokens = jnp.stack(token_grads)[None]
    return (
        query_loss,
        grad_tokens,
        running[0],
        running[1],
        running[2],
        running[3],
        running[4],
        running[5],
        running[6],
        running[7],
        running[8],
        running[9],
    )


def solution(mesh):
    return jax.shard_map(
        local,
        mesh=mesh,
        in_specs=(
            P("tower", None, ("dp", "fsdp"), None, None),
            P(None, ("dp", "fsdp"), None),
            P(None, ("dp", "fsdp"), None),
            P("fsdp"),
            P("fsdp"),
            P("fsdp", None),
            P("fsdp", None),
            P("fsdp", None),
            P("fsdp", None),
            P("fsdp", None),
            P("fsdp", None),
            P("fsdp", None),
            P("fsdp", None),
        ),
        out_specs=(
            P(None, ("dp", "fsdp"), None),
            P("tower", None, ("dp", "fsdp"), None, None),
            P("fsdp"),
            P("fsdp"),
            P("fsdp", None),
            P("fsdp", None),
            P("fsdp", None),
            P("fsdp", None),
            P("fsdp", None),
            P("fsdp", None),
            P("fsdp", None),
            P("fsdp", None),
        ),
        check_vma=False,
    )
```

profile of v0, /device:TPU:0, one launch (start us, length us, event | category | flops | bytes accessed | tf_op | source)
XLA Modules:
  0.0 1102.9 jit_solution(14041247499464607919)
XLA Ops:
  20.7 8.5 all-reduce.16
  35.9 9.7 fusion.2
  45.6 17.8 %copy.96 = f32[512,512,12]{0,1,2:T(8,128)} copy(f32[512,512,12]{1,2,0:T(8,128)} %fusion.2) | data formatting | bytes 25165824 | tf_op jit(solution)/shard_map/ijb,bh->hij/dot_general | solution.py:229
  135.7 32.5 %all-gather.20.cloned.1.call-done = bf16[3072,768]{1,0:T(8,128)(2,1)} async-done(((bf16[768,768]{1,0:T(8,128)(2,1)}), bf16[3072,768]{1,0:T(8,128)(2,1)}) %all-gather.20.cloned.1.call-update) | async-done | bytes 4718608 | tf_op jit(solution)/shard_map/all_gather | solution.py:213
  168.2 7.2 fusion.190
  176.4 11.5 %all-gather.22.cloned.1.call-done = bf16[768,768]{1,0:T(8,128)(2,1)} async-done(((bf16[192,768]{1,0:T(8,128)(2,1)}), bf16[768,768]{1,0:T(8,128)(2,1)}) %all-gather.22.cloned.1.call-update) | async-done | bytes 1179664 | tf_op jit(solution)/shard_map/all_gather | solution.py:214
  212.0 20.5 %all-gather = bf16[16,1,768]{2,1,0:T(2,128)(2,1)S(1)} all-gather(bf16[1,1,768]{2,1,0:T(2,128)(2,1)S(1)} %fusion.149), channel_id=1, replica_groups=mesh['tower'=2,'dp'=4,'fsdp'=4] {'dp','fsdp'}, dimensions={0}, use_global_device_ids=true | all-gather | bytes 26112 | tf_op jit(solution)/shard_map/all_gather | solution.py:293
  232.5 17.5 %all-gather.1 = bf16[16,1,768]{2,1,0:T(2,128)(2,1)S(1)} all-gather(bf16[1,1,768]{2,1,0:T(2,128)(2,1)S(1)} %fusion.150), channel_id=1, replica_groups=mesh['tower'=2,'dp'=4,'fsdp'=4] {'dp','fsdp'}, dimensions={0}, use_global_device_ids=true | all-gather | bytes 26112 | tf_op jit(solution)/shard_map/all_gather | solution.py:293
  254.2 84.4 %all-reduce.20.cloned.1.call-done = (f32[16,768]{1,0:T(8,128)}, f32[16,768]{1,0:T(8,128)}) async-done(((f32[16,768]{1,0:T(8,128)}, f32[16,768]{1,0:T(8,128)}), (f32[16,768]{1,0:T(8,128)}, f32[16,768]{1,0:T(8,128)})) %all-reduce.20.cloned.1.call-update) | async-done | bytes 98320
  351.2 9.5 fusion.18
  360.8 9.9 fusion.25
  390.4 7.1 fusion.72
  405.8 7.1 fusion.75
  416.1 7.9 multiply_reduce_fusion.1
  436.9 7.9 multiply_reduce_fusion
  474.5 8.8 convolution_convert_fusion.1
  483.3 8.8 convolution_convert_fusion
  492.1 7.3 convolution_convert_fusion.3
  511.9 25.6 %reduce-scatter.15.cloned.1.call-done = bf16[192,768]{1,0:T(8,128)(2,1)} async-done(((bf16[768,768]{1,0:T(8,128)(2,1)}), bf16[192,768]{1,0:T(8,128)(2,1)}) %reduce-scatter.15.cloned.1.call-update) | async-done | bytes 294928 | tf_op jit(solution)/shard_map/reduce_scatter | solution.py:147
  537.4 28.2 %reduce-scatter.17.cloned.1.call-done = bf16[192,768]{1,0:T(8,128)(2,1)} async-done(((bf16[768,768]{1,0:T(8,128)(2,1)}), bf16[192,768]{1,0:T(8,128)(2,1)}) %reduce-scatter.17.cloned.1.call-update) | async-done | bytes 294928 | tf_op jit(solution)/shard_map/reduce_scatter | solution.py:147
  567.5 26.4 %reduce-scatter.19.cloned.1.call-done = bf16[192,768]{1,0:T(8,128)(2,1)} async-done(((bf16[768,768]{1,0:T(8,128)(2,1)}), bf16[192,768]{1,0:T(8,128)(2,1)}) %reduce-scatter.19.cloned.1.call-update) | async-done | bytes 294928 | tf_op jit(solution)/shard_map/reduce_scatter | solution.py:150
  593.9 28.2 %reduce-scatter.21.cloned.1.call-done = bf16[192,768]{1,0:T(8,128)(2,1)} async-done(((bf16[768,768]{1,0:T(8,128)(2,1)}), bf16[192,768]{1,0:T(8,128)(2,1)}) %reduce-scatter.21.cloned.1.call-update) | async-done | bytes 294928 | tf_op jit(solution)/shard_map/reduce_scatter | solution.py:150
  624.0 48.6 %reduce-scatter.35.cloned.1.call-done = bf16[768,768]{1,0:T(8,128)(2,1)} async-done(((bf16[3072,768]{1,0:T(8,128)(2,1)}), bf16[768,768]{1,0:T(8,128)(2,1)}) %reduce-scatter.35.cloned.1.call-update) | async-done | bytes 1179664 | tf_op jit(solution)/shard_map/reduce_scatter | solution.py:165
  672.7 50.3 %reduce-scatter.37.cloned.1.call-done = bf16[768,768]{1,0:T(8,128)(2,1)} async-done(((bf16[3072,768]{1,0:T(8,128)(2,1)}), bf16[768,768]{1,0:T(8,128)(2,1)}) %reduce-scatter.37.cloned.1.call-update) | async-done | bytes 1179664 | tf_op jit(solution)/shard_map/reduce_scatter | solution.py:165
  726.2 47.3 %reduce-scatter.31.cloned.1.call-done = bf16[192,3072]{1,0:T(8,128)(2,1)} async-done(((bf16[768,3072]{1,0:T(8,128)(2,1)}), bf16[192,3072]{1,0:T(8,128)(2,1)}) %reduce-scatter.31.cloned.1.call-update) | async-done | bytes 1179664 | tf_op jit(solution)/shard_map/reduce_scatter | solution.py:162
  773.5 50.4 %reduce-scatter.33.cloned.1.call-done = bf16[192,3072]{1,0:T(8,128)(2,1)} async-done(((bf16[768,3072]{1,0:T(8,128)(2,1)}), bf16[192,3072]{1,0:T(8,128)(2,1)}) %reduce-scatter.33.cloned.1.call-update) | async-done | bytes 1179664 | tf_op jit(solution)/shard_map/reduce_scatter | solution.py:162
  829.2 14.8 %copy.110 = bf16[12,512,512]{2,0,1:T(8,128)(2,1)} copy(bf16[12,512,512]{1,2,0:T(8,128)(2,1)} %copy-done.2) | data formatting | bytes 12582912 | tf_op jit(solution)/shard_map/while/body/eval_jaxpr/convert_element_type | solution.py:116
  843.9 14.5 %copy.111 = bf16[12,512,512]{2,0,1:T(8,128)(2,1)} copy(bf16[12,512,512]{1,2,0:T(8,128)(2,1)} %copy-done.3) | data formatting | bytes 12582912 | tf_op jit(solution)/shard_map/while/body/eval_jaxpr/convert_element_type | solution.py:116
  869.2 7.3 fusion.93
  883.4 11.1 %all-reduce.15 = (bf16[768]{0:T(1024)(128)(2,1)S(1)}, bf16[768]{0:T(1024)(128)(2,1)S(1)}, bf16[768]{0:T(1024)(128)(2,1)S(1)}, bf16[768]{0:T(1024)(128)(2,1)S(1)}...) all-reduce(bf16[768]{0:T(1024)(128)(2,1)S(1)} %get-tuple-element.19, ...), channel_id=5, replica_groups=mesh['tower'=2,'dp'=4,'fsdp'=4] {'fsdp'}, use_global_device_ids=true, to_apply=%region_34.35.clone | all-reduce | flops 3840 | bytes 15360
  894.6 24.2 %all-reduce.13 = (f32[192]{0:T(256)}, f32[192]{0:T(256)}, f32[8,12]{1,0:T(8,128)}) all-reduce(f32[192]{0:T(256)S(1)} %convert_add_fusion.9, f32[192]{0:T(256)S(1)} %convert_add_fusion.8, f32[8,12]{1,0:T(8,128)S(1)} %convert_add_fusion.7), channel_id=1, replica_groups=mesh['tower'=2,'dp'=4,'fsdp'=4] {'tower','dp'}, use_global_device_ids=true, to_apply=%region_32.33 | all-reduce | flops 480 | bytes 3840 | tf_op jit(solution)/shard_map/psum | solution.py:172
  923.3 163.6 %all-reduce.22.cloned.1.call-done = (f32[192,768]{1,0:T(8,128)}, f32[192,768]{1,0:T(8,128)}, f32[192,768]{1,0:T(8,128)}, f32[192,768]{1,0:T(8,128)}, f32[192,307...) async-done(((f32[192,768]{1,0:T(8,128)}, f32[192,768]{1,0:T(8,128)}, f32[192,768]{1,0:T(8,128)}, f32[192,768]{1,0:T(8,128)}, f32[192,3072]{1,0:T(8,128)}, ...) | async-done | bytes 7667728 | tf_op jit(solution)/shard_map/psum | solution.py:172
  (378 shorter events, 261.1 us)
Async XLA Ops:
  7.2 56.2 %all-gather.10.cloned.1.call-start = ((), (), s32[]{:S(2)}) async-start(), calls=%async_computation.14 | async-start | bytes 1474560 | tf_op jit(solution)/shard_map/all_gather | solution.py:209
  9.2 63.7 %all-gather.14.cloned.1.call-start = ((), (), s32[]{:S(2)}) async-start(), calls=%async_computation.16 | async-start | bytes 1474560 | tf_op jit(solution)/shard_map/all_gather | solution.py:208
  10.0 70.0 %all-gather.12.cloned.1.call-start = ((), (), s32[]{:S(2)}) async-start(), calls=%async_computation.15 | async-start | bytes 1474560 | tf_op jit(solution)/shard_map/all_gather | solution.py:207
  10.8 94.1 %all-gather.16.cloned.1.call-start = ((), (), s32[]{:S(2)}) async-start(), calls=%async_computation.17 | async-start | bytes 1474560 | tf_op jit(solution)/shard_map/all_gather | solution.py:210
  12.7 116.0 %all-gather.18.cloned.1.call-start = ((), (), s32[]{:S(2)}) async-start(), calls=%async_computation.18 | async-start | bytes 5898240 | tf_op jit(solution)/shard_map/all_gather | solution.py:212
  14.0 154.2 %all-gather.20.cloned.1.call-start = ((), (), s32[]{:S(2)}) async-start(), calls=%async_computation.19 | async-start | bytes 5898240 | tf_op jit(solution)/shard_map/all_gather | solution.py:213
  17.0 170.9 %all-gather.22.cloned.1.call-start = ((), (), s32[]{:S(2)}) async-start(), calls=%async_computation.20 | async-start | bytes 1474560 | tf_op jit(solution)/shard_map/all_gather | solution.py:214
  17.8 320.8 %all-reduce.20.cloned.1.call-start = ((), (), s32[]{:S(2)}) async-start(), calls=%async_computation.35 | async-start | bytes 196608
  18.4 232.4 %copy-start.63 = (s32[8]{0:T(128)}, s32[8]{0:T(128)S(1)}, u32[]{:S(2)}) copy-start(s32[8]{0:T(128)S(1)} %get-tuple-element.230) | copy-start | bytes 100
  80.0 27.8 %copy-start.7 = (bf16[512,768]{0,1:T(8,128)(2,1)}, bf16[512,768]{0,1:T(8,128)(2,1)S(1)}, u32[]{:S(2)}) copy-start(bf16[512,768]{0,1:T(8,128)(2,1)S(1)} %copy.95) | copy-start | bytes 2359300
  121.8 53.7 %copy-start.27 = (f32[512,768]{1,0:T(8,128)}, f32[512,768]{1,0:T(8,128)S(1)}, u32[]{:S(2)}) copy-start(f32[512,768]{1,0:T(8,128)S(1)} %get-tuple-element.248) | copy-start | bytes 4718596
  199.7 54.0 %copy-start.70 = (u32[32]{0:T(128)S(1)}, u32[32]{0:T(128)}, u32[]{:S(2)}) copy-start(u32[32]{0:T(128)} %constant.199) | copy-start | bytes 388
  200.2 11.7 %collective-permute-start.1 = (bf16[1,768]{1,0:T(2,128)(2,1)S(1)}, bf16[1,768]{1,0:T(2,128)(2,1)S(1)}, u32[]{:S(2)}, u32[]{:S(2)}) collective-permute-start(bf16[1,768]{1,0:T(2,128)(2,1)S(1)} %slice_bitcast_fusion.1), channel_id=1, source_target_pairs={{16,0},{17,1},{18,2},{19,3},{20,4},{21,5},{22,6},{23,7},{24,8},{25... | collective-permute-start | bytes 4616 | tf_op jit(solution)/shard_map/ppermute | solution.py:29
  201.5 48.6 %collective-permute-start = (bf16[8,768]{1,0:T(8,128)(2,1)S(1)}, bf16[8,768]{1,0:T(8,128)(2,1)S(1)}, u32[]{:S(2)}, u32[]{:S(2)}) collective-permute-start(bf16[8,768]{1,0:T(8,128)(2,1)S(1)} %multiply_convert_fusion.7), channel_id=1, source_target_pairs={{0,16},{1,17},{2,18},{3,19},{4,20},{5,21},{6,22},{7,23},{8,24},{9,... | collective-permute-start | bytes 36872 | tf_op jit(solution)/shard_map/ppermute | solution.py:29
  206.1 5.9 collective-permute-start.3
  207.4 43.2 %collective-permute-start.2 = (bf16[8,768]{1,0:T(8,128)(2,1)S(1)}, bf16[8,768]{1,0:T(8,128)(2,1)S(1)}, u32[]{:S(2)}, u32[]{:S(2)}) collective-permute-start(bf16[8,768]{1,0:T(8,128)(2,1)S(1)} %multiply_convert_fusion.6), channel_id=1, source_target_pairs={{0,16},{1,17},{2,18},{3,19},{4,20},{5,21},{6,22},{7,23},{8,24},{9,... | collective-permute-start | bytes 36872 | tf_op jit(solution)/shard_map/ppermute | solution.py:29
  253.6 252.5 %reduce-scatter.41.cloned.1.call-start = ((), (), s32[]{:S(2)}) async-start(), calls=%async_computation.34 | async-start | bytes 1474560 | tf_op jit(solution)/shard_map/reduce_scatter | solution.py:168
  342.7 163.4 %reduce-scatter.39.cloned.1.call-start = ((), (), s32[]{:S(2)}) async-start(), calls=%async_computation.33 | async-start | bytes 1474560 | tf_op jit(solution)/shard_map/reduce_scatter | solution.py:168
  351.1 156.9 %reduce-scatter.29.cloned.1.call-start = ((), (), s32[]{:S(2)}) async-start(), calls=%async_computation.28 | async-start | bytes 1474560 | tf_op jit(solution)/shard_map/reduce_scatter | solution.py:156
  380.8 127.2 %reduce-scatter.27.cloned.1.call-start = ((), (), s32[]{:S(2)}) async-start(), calls=%async_computation.27 | async-start | bytes 1474560 | tf_op jit(solution)/shard_map/reduce_scatter | solution.py:156
  384.3 125.6 %reduce-scatter.23.cloned.1.call-start = ((), (), s32[]{:S(2)}) async-start(), calls=%async_computation.25 | async-start | bytes 1474560 | tf_op jit(solution)/shard_map/reduce_scatter | solution.py:153
  400.4 109.6 %reduce-scatter.25.cloned.1.call-start = ((), (), s32[]{:S(2)}) async-start(), calls=%async_computation.26 | async-start | bytes 1474560 | tf_op jit(solution)/shard_map/reduce_scatter | solution.py:153
  415.8 121.7 %reduce-scatter.15.cloned.1.call-start = ((), (), s32[]{:S(2)}) async-start(), calls=%async_computation.21 | async-start | bytes 1474560 | tf_op jit(solution)/shard_map/reduce_scatter | solution.py:147
  436.9 128.7 %reduce-scatter.17.cloned.1.call-start = ((), (), s32[]{:S(2)}) async-start(), calls=%async_computation.22 | async-start | bytes 1474560 | tf_op jit(solution)/shard_map/reduce_scatter | solution.py:147
  457.5 136.5 %reduce-scatter.19.cloned.1.call-start = ((), (), s32[]{:S(2)}) async-start(), calls=%async_computation.23 | async-start | bytes 1474560 | tf_op jit(solution)/shard_map/reduce_scatter | solution.py:150
  466.3 155.8 %reduce-scatter.21.cloned.1.call-start = ((), (), s32[]{:S(2)}) async-start(), calls=%async_computation.24 | async-start | bytes 1474560 | tf_op jit(solution)/shard_map/reduce_scatter | solution.py:150
  474.4 198.2 %reduce-scatter.35.cloned.1.call-start = ((), (), s32[]{:S(2)}) async-start(), calls=%async_computation.31 | async-start | bytes 5898240 | tf_op jit(solution)/shard_map/reduce_scatter | solution.py:165
  483.3 239.7 %reduce-scatter.37.cloned.1.call-start = ((), (), s32[]{:S(2)}) async-start(), calls=%async_computation.32 | async-start | bytes 5898240 | tf_op jit(solution)/shard_map/reduce_scatter | solution.py:165
  492.1 281.4 %reduce-scatter.31.cloned.1.call-start = ((), (), s32[]{:S(2)}) async-start(), calls=%async_computation.29 | async-start | bytes 5898240 | tf_op jit(solution)/shard_map/reduce_scatter | solution.py:162
  499.5 324.4 %reduce-scatter.33.cloned.1.call-start = ((), (), s32[]{:S(2)}) async-start(), calls=%async_computation.30 | async-start | bytes 5898240 | tf_op jit(solution)/shard_map/reduce_scatter | solution.py:162
  506.0 580.9 %all-reduce.22.cloned.1.call-start = ((), (), s32[]{:S(2)}) async-start(), calls=%async_computation.36 | async-start | bytes 15335424 | tf_op jit(solution)/shard_map/psum | solution.py:172
  876.6 42.2 %copy-start.13 = (f32[512,768]{1,0:T(8,128)S(1)}, f32[512,768]{1,0:T(8,128)}, u32[]{:S(2)}) copy-start(f32[512,768]{1,0:T(8,128)} %get-tuple-element.228) | copy-start | bytes 4718596
  (76 other events, 349.1 us)
Sparse Core Ops, SparseCore 0:
  10.2 20.2 all-gather.9
  32.6 17.4 all-gather.13
  52.3 17.4 all-gather.11
  71.7 17.4 all-gather.15
  91.2 37.4 all-gather.17
  130.7 37.4 all-gather.19
  170.4 17.4 all-gather.21
  253.7 84.8 all-reduce.19
  342.8 24.6 reduce-scatter.40
  369.9 25.7 reduce-scatter.38
  398.4 25.7 reduce-scatter.28
  426.6 25.7 reduce-scatter.26
  455.1 25.7 reduce-scatter.22
  483.4 25.7 reduce-scatter.24
  511.7 25.6 reduce-scatter.14
  539.9 25.7 reduce-scatter.16
  568.2 25.7 reduce-scatter.18
  596.4 25.7 reduce-scatter.20
  624.8 47.8 reduce-scatter.34
  675.1 47.8 reduce-scatter.36
  725.6 47.8 reduce-scatter.30
  776.1 47.8 reduce-scatter.32
  831.5 255.3 all-reduce.21
where the time goes:
time: 1110 us; the launch traced here: 1100 us
  waiting for transfers between devices  604 us (54%)
  matrix products  233 us (21%)
  local copies, waits for them, and re-layouts  94.4 us (9%)
  blocking collectives  87 us (8%)
  other arithmetic  53 us (5%)
  between operations  17.5 us (2%)
  starting transfers between devices  13.5 us (1%)
    psum x1, waiting for transfers between devices, reduce_now(): lax.psum((shards[0], shards[1], shards[2], shards[3], shards[4], shards[5...  164 us
    reduce_scatter x2, waiting for transfers between devices, reduce_now(): lax.psum_scatter(gradients[8].astype(jnp.bfloat16), 'fsdp', scatter_dimen...  98.9 us
    reduce_scatter x2, waiting for transfers between devices, reduce_now(): lax.psum_scatter(gradients[7].astype(jnp.bfloat16), 'fsdp', scatter_dimen...  97.7 us
    unnamed x24, waiting for transfers between devices  84.8 us
    reduce_scatter x2, waiting for transfers between devices, reduce_now(): lax.psum_scatter(gradients[3].astype(jnp.bfloat16), 'fsdp', scatter_dimen...  54.6 us
    reduce_scatter x2, waiting for transfers between devices, reduce_now(): lax.psum_scatter(gradients[2].astype(jnp.bfloat16), 'fsdp', scatter_dimen...  53.7 us
    all_gather x2, blocking collectives, local(): lax.all_gather(passage_local, ('dp', 'fsdp'), axis=0, tiled=True)  38.1 us
    all_gather x1, waiting for transfers between devices, local(): lax.all_gather(w_ffn_out.astype(jnp.bfloat16), 'fsdp', axis=0, tiled=True)  32.5 us
  transfers between devices with their start and end apart: 27, of which 13 were waited for; matrix products, arithmetic and copies ran while one was open for 30% of the time, Pallas kernels for 0%

commit v1 on v0

v1 whole, which is shorter than its diff:
```python
import functools

import jax
import jax.numpy as jnp
from jax import lax
from jax.experimental import pallas as pl
from jax.experimental.pallas import tpu as pltpu
from jax.sharding import PartitionSpec as P

D = 768
H = 12
DH = 64
FF = 3072
NB = 32
SEQ = 512
QSEG = 8
MB = 2
T = MB * SEQ
SLOTS = MB * QSEG
PAY = D + 128
EPSILON = 1e-06
LOGIT_SCALE = 50.0
LOSS_SCALE = 256.0
THRESHOLDS = (12, 16, 23, 32, 46, 64, 91)
GELU_C = 0.7978845608028654
ALL = ("tower", "dp", "fsdp")
BF = jnp.bfloat16
F32 = jnp.float32
HIGHEST = lax.Precision.HIGHEST
NT = (((1,), (1,)), ((), ()))
TN = (((0,), (0,)), ((), ()))

def bucket_of(m):
    a=jnp.abs(m)
    far=8+sum((a>=t).astype(jnp.int32) for t in THRESHOLDS)
    return jnp.where(m>0,16,0)+jnp.where(a<8,a,far)

def diag_hot():
    col=lax.broadcasted_iota(jnp.int32,(NB,1024),1)
    m=(col//128-3)*128-col%128
    return (bucket_of(m)==lax.broadcasted_iota(jnp.int32,(NB,1024),0)).astype(BF)

def bias_kernel(tab_ref, hot_ref, out_ref):
    w=jnp.dot(tab_ref[...],hot_ref[...],preferred_element_type=F32)
    jj=lax.broadcasted_iota(jnp.int32,(128,128),0); ii=lax.broadcasted_iota(jnp.int32,(128,128),1)
    up=ii>=jj
    for h in range(H):
        prev=None
        for e in range(8):
            r=pltpu.roll(jnp.broadcast_to(w[h:h+1,e*128:(e+1)*128],(128,128)),0,1,stride=1,stride_axis=0)
            if e>0: out_ref[h,e-1]=jnp.where(up,prev,r)
            prev=r
def bias_blocks(table_t, hot):
    return pl.pallas_call(bias_kernel,out_shape=jax.ShapeDtypeStruct((H,7,128,128),F32),name="bias_blocks")(table_t,hot)

def attn_fwd_kernel(q_ref,k_ref,v_ref,fq_ref,fk_ref,bias_ref,o_ref,ot_ref,e_ref,li_ref):
    lane=lax.broadcasted_iota(jnp.int32,(SEQ,128),1)
    q=q_ref[...];k=k_ref[...];fq=fq_ref[...];fk=fk_ref[...]
    vt=v_ref[...].T
    outs=[]
    for s in range(2):
        own=(lane<64) if s==0 else (lane>=64)
        qa=jnp.where(own,q,fq); ka=jnp.where(own,k,fk)
        st=lax.dot_general(ka,qa,(((1,),(1,)),((),())),preferred_element_type=F32)
        b=jnp.concatenate([jnp.concatenate([bias_ref[s,bj-bi+3] for bi in range(4)],axis=1) for bj in range(4)],axis=0)
        st=st+b
        top=jnp.max(st,axis=0,keepdims=True)
        e=jnp.exp(st-top).astype(BF)
        e_ref[0,s]=e
        va=jnp.concatenate([vt[64*s:64*s+64],jnp.ones((16,SEQ),BF)],axis=0)
        ot=jnp.dot(va,e,preferred_element_type=F32)
        linv=1.0/ot[64:65]
        li_ref[0,s]=jnp.broadcast_to(linv,(8,SEQ))
        outs.append((ot[:64]*linv).astype(BF))
    ot=jnp.concatenate(outs,axis=0)
    ot_ref[...]=ot
    o_ref[...]=ot.T

def attn_fwd(qkv,fq,fk,bias):
    grid=(6,2)
    return pl.pallas_call(attn_fwd_kernel,grid=grid,
      in_specs=[pl.BlockSpec((SEQ,128),lambda p,r:(r,p)),pl.BlockSpec((SEQ,128),lambda p,r:(r,6+p)),pl.BlockSpec((SEQ,128),lambda p,r:(r,12+p)),
        pl.BlockSpec((SEQ,128),lambda p,r:(r,0)),pl.BlockSpec((SEQ,128),lambda p,r:(r,0)),
        pl.BlockSpec((2,7,128,128),lambda p,r:(p,0,0,0))],
      out_specs=[pl.BlockSpec((SEQ,128),lambda p,r:(r,p)),pl.BlockSpec((128,SEQ),lambda p,r:(p,r)),
        pl.BlockSpec((1,2,SEQ,SEQ),lambda p,r:(r,p,0,0)),pl.BlockSpec((1,2,8,SEQ),lambda p,r:(r,p,0,0))],
      out_shape=[jax.ShapeDtypeStruct((T,D),BF),jax.ShapeDtypeStruct((D,T),BF),jax.ShapeDtypeStruct((2,H,SEQ,SEQ),BF),jax.ShapeDtypeStruct((2,H,8,SEQ),F32)],
      compiler_params=pltpu.CompilerParams(dimension_semantics=("arbitrary","arbitrary"),vmem_limit_bytes=48*2**20),name="attn_fwd")(qkv,qkv,qkv,fq,fk,bias)

def attn_bwd_kernel(q_ref,k_ref,v_ref,do_ref,ot_ref,e_ref,li_ref,dq_ref,dk_ref,dv_ref,diag_ref,acc):
    r=pl.program_id(1)
    lane=lax.broadcasted_iota(jnp.int32,(SEQ,128),1)
    q=q_ref[...];k=k_ref[...];v=v_ref[...];do=do_ref[...]
    kt=k.T
    dot_=do.T
    dqs=[]
    prod=dot_.astype(F32)*ot_ref[...].astype(F32)
    for s in range(2):
        own=(lane<64) if s==0 else (lane>=64)
        linv=li_ref[0,s,0:1,:]
        delta=jnp.sum(prod[64*s:64*s+64],axis=0,keepdims=True)
        vm=jnp.where(own,v,jnp.zeros_like(v))
        dp=lax.dot_general(vm,do,(((1,),(1,)),((),())),preferred_element_type=F32)
        p=e_ref[0,s].astype(F32)*linv
        ds32=p*(dp-delta)
        ds=ds32.astype(BF)
        pb=p.astype(BF)
        dvh=jnp.dot(pb,do,preferred_element_type=F32)
        dkh=jnp.dot(ds,q,preferred_element_type=F32)
        dqt=jnp.dot(kt[64*s:64*s+64],ds,preferred_element_type=F32)
        dqs.append(dqt.astype(BF))
        if s==0: dv0,dk0=dvh,dkh
        else:
            dv_ref[...]=jnp.where(lane<64,dv0,dvh).astype(BF)
            dk_ref[...]=jnp.where(lane<64,dk0,dkh).astype(BF)
        sums=[]
        for d in range(-3,4):
            t=None
            for bj in range(4):
                bi=bj-d
                if 0<=bi<4:
                    blk=ds32[128*bj:128*bj+128,128*bi:128*bi+128]
                    t=blk if t is None else t+blk
            sums.append(t)
        for d in range(7):
            prev=jnp.where(r==0,jnp.zeros((128,128),F32),acc[s,d])
            acc[s,d]=prev+sums[d]
    dq_ref[...]=jnp.concatenate(dqs,axis=0).T
    @pl.when(r==1)
    def _():
        jj=lax.broadcasted_iota(jnp.int32,(128,128),0); ii=lax.broadcasted_iota(jnp.int32,(128,128),1)
        up=ii>=jj
        for s in range(2):
            rows=[]
            for e in range(8):
                a=acc[s,e] if e<7 else jnp.zeros((128,128),F32)
                b=acc[s,e-1] if e>0 else jnp.zeros((128,128),F32)
                c=jnp.where(up,a,b)
                t=c[0:8]
                for g in range(1,16):
                    t=t+pltpu.roll(c[8*g:8*g+8],128-8*g,1)
                rows.append(t)
            diag_ref[0,s]=jnp.concatenate(rows,axis=1)

def diag_hot2():
    c=lax.broadcasted_iota(jnp.int32,(8192,NB),0)
    s=c//1024; col=c%1024
    m=(col//128-3)*128-(col%128-s)%128
    return (bucket_of(m)==lax.broadcasted_iota(jnp.int32,(8192,NB),1)).astype(F32)

def attn_bwd(qkv,do,ot,e,li):
    return pl.pallas_call(attn_bwd_kernel,grid=(6,2),
      in_specs=[pl.BlockSpec((SEQ,128),lambda p,r:(r,p)),pl.BlockSpec((SEQ,128),lambda p,r:(r,6+p)),pl.BlockSpec((SEQ,128),lambda p,r:(r,12+p)),
        pl.BlockSpec((SEQ,128),lambda p,r:(r,p)),pl.BlockSpec((128,SEQ),lambda p,r:(p,r)),
        pl.BlockSpec((1,2,SEQ,SEQ),lambda p,r:(r,p,0,0)),pl.BlockSpec((1,2,8,SEQ),lambda p,r:(r,p,0,0))],
      out_specs=[pl.BlockSpec((SEQ,128),lambda p,r:(r,p))]*3+[pl.BlockSpec((1,2,8,1024),lambda p,r:(p,0,0,0))],
      out_shape=[jax.ShapeDtypeStruct((T,D),BF)]*3+[jax.ShapeDtypeStruct((6,2,8,1024),F32)],
      scratch_shapes=[pltpu.VMEM((2,7,128,128),F32)],
      compiler_params=pltpu.CompilerParams(dimension_semantics=("arbitrary","arbitrary"),vmem_limit_bytes=48*2**20),name="attn_bwd")(qkv,qkv,qkv,do,ot,e,li)


def swap(block, axis, bit):
    size = lax.axis_size(axis)
    return lax.ppermute(block, axis, [(i, i ^ bit) for i in range(size)])


def gather_group(shard):
    rows, cols = shard.shape
    half = rows // 2
    f = lax.axis_index("fsdp")
    t = lax.axis_index("tower")
    sent = lax.dynamic_slice_in_dim(shard, t * half, half, 0)
    near = swap(sent, "fsdp", 2)
    mate = swap(shard, "fsdp", 1)
    far = swap(near, "tower", 1)
    near_mate = swap(near, "fsdp", 1)
    far_mate = swap(far, "fsdp", 1)
    full = jnp.zeros((4 * rows, cols), shard.dtype)
    for piece, start in (
        (shard, f * rows),
        (mate, (f ^ 1) * rows),
        (near, (f ^ 2) * rows + t * half),
        (far, (f ^ 2) * rows + (1 - t) * half),
        (near_mate, (f ^ 3) * rows + t * half),
        (far_mate, (f ^ 3) * rows + (1 - t) * half),
    ):
        full = lax.dynamic_update_slice_in_dim(full, piece, start, 0)
    return full


def pick(parts, index):
    return lax.dynamic_index_in_dim(parts, index, 0, keepdims=False)


def added(kept, got):
    return lax.optimization_barrier((kept.astype(F32) + got.astype(F32)).astype(BF))


def reduce_group(grads):
    rows, cols = grads.shape
    quarter = rows // 4
    f = lax.axis_index("fsdp")
    a, b = f // 2, f % 2
    t = lax.axis_index("tower")
    parts = grads.reshape(2, 2, quarter, cols)
    sent = lax.dynamic_index_in_dim(parts, 1 - b, 1, keepdims=False)
    kept = lax.dynamic_index_in_dim(parts, b, 1, keepdims=False)
    total = added(kept, swap(sent, "fsdp", 1))
    total = added(pick(total, a), swap(pick(total, 1 - a), "fsdp", 2))
    total = total.reshape(2, quarter // 2, cols)
    total = added(pick(total, t), swap(pick(total, 1 - t), "tower", 1))
    bit = 1
    while bit < lax.axis_size("dp"):
        total = added(total, swap(total, "dp", bit))
        bit *= 2
    other = swap(total, "tower", 1)
    first = jnp.where(t == 0, total, other)
    second = jnp.where(t == 0, other, total)
    return jnp.concatenate([first, second], axis=0).astype(F32)


def loss_kernel(rows, pos_ref, buf_ref, proj_ref, loss_ref, own_ref, all_ref, gproj_ref, scr, gp_scr, sem):
    me, is_query, row, quarter = pos_ref[0], pos_ref[1], pos_ref[2], pos_ref[3]
    nq, np_ = rows * SLOTS, rows * MB
    for k in range(2 * rows):
        a = me ^ k
        start = ((a >> 2) & 1) * nq + ((a >> 3) * 4 + (a & 3)) * SLOTS
        pltpu.make_async_copy(
            buf_ref.at[pl.ds(k * SLOTS, SLOTS)], scr.at[pl.ds(pl.multiple_of(start, SLOTS), SLOTS)], sem
        ).start()
    pltpu.make_async_copy(buf_ref, scr, sem).wait()
    picker = (
        lax.broadcasted_iota(jnp.int32, (np_, nq), 1) == QSEG * lax.broadcasted_iota(jnp.int32, (np_, nq), 0)
    ).astype(BF)
    q_all = scr[:nq]
    p_all = jnp.dot(picker, scr[nq:], preferred_element_type=F32).astype(BF)
    both = jnp.concatenate([q_all[:, :D], p_all[:, :D]], axis=0)
    extra = jnp.concatenate([q_all[:, D:], p_all[:, D:]], axis=0).astype(F32)
    z = jnp.dot(both, proj_ref[...], preferred_element_type=F32)
    inv = lax.rsqrt(jnp.sum(z * z, axis=-1, keepdims=True) + EPSILON)
    w = z * inv
    e = w.astype(BF)
    eq, ep = e[:nq], e[nq:]
    logits = LOGIT_SCALE * lax.dot_general(eq, ep, NT, preferred_element_type=F32)
    q_row = lax.broadcasted_iota(jnp.int32, (nq, np_), 0)
    p_col = lax.broadcasted_iota(jnp.int32, (nq, np_), 1)
    micro = (q_row // QSEG) % MB
    same = micro == p_col % MB
    logits = jnp.where(same, logits, -1e30)
    top = jnp.max(logits, axis=-1, keepdims=True)
    log_total = top + jnp.log(jnp.sum(jnp.exp(logits - top), axis=-1, keepdims=True))
    positive = extra[:nq, 1:2].astype(jnp.int32)
    hot = jnp.where(same & (p_col // MB == positive), 1.0, 0.0)
    chosen = jnp.sum(logits * hot, axis=-1, keepdims=True)
    loss = log_total - chosen
    gl = LOSS_SCALE * (jnp.exp(logits - log_total) - hot)
    g_eq = LOGIT_SCALE * jnp.dot(gl, ep.astype(F32), precision=HIGHEST, preferred_element_type=F32)
    g_ep = LOGIT_SCALE * lax.dot_general(gl, eq.astype(F32), TN, precision=HIGHEST, preferred_element_type=F32)
    ge = jnp.concatenate([g_eq, g_ep], axis=0)
    gz = (inv * (ge - w * jnp.sum(w * ge, axis=-1, keepdims=True))).astype(BF)
    gp_scr[...] = lax.dot_general(both, gz, TN, preferred_element_type=F32)
    gproj_ref[...] = gp_scr[pl.ds(pl.multiple_of(quarter * (D // 4), D // 4), D // 4), :]
    g_pooled = lax.dot_general(gz, proj_ref[...], NT, preferred_element_type=F32)
    g_x3 = g_pooled / jnp.maximum(extra[:, 0:1], 1.0)
    gp3 = jnp.concatenate([g_x3[nq:]], axis=0)
    hi = gp3.astype(BF)
    lo = (gp3 - hi.astype(F32)).astype(BF)
    spread = lambda v: lax.dot_general(picker, v, TN, preferred_element_type=F32)
    all_ref[0] = g_x3[:nq].astype(BF)
    p_hi = spread(hi)
    all_ref[1] = p_hi.astype(BF)
    p_full = p_hi + spread(lo)
    scr_q = jnp.where(is_query == 1, g_x3[:nq], p_full)
    gp_big = scr_q
    own_sel = (
        lax.broadcasted_iota(jnp.int32, (SLOTS, nq), 1) == row * SLOTS + lax.broadcasted_iota(jnp.int32, (SLOTS, nq), 0)
    ).astype(F32)
    own_ref[...] = jnp.dot(own_sel, gp_big, precision=HIGHEST, preferred_element_type=F32)
    loss_ref[...] = jnp.dot(
        own_sel, jnp.broadcast_to(loss, (nq, 128)), precision=HIGHEST, preferred_element_type=F32
    )


def loss_call(place, buf, proj, rows):
    nq = rows * SLOTS
    return pl.pallas_call(
        functools.partial(loss_kernel, rows),
        in_specs=[
            pl.BlockSpec(memory_space=pltpu.SMEM),
            pl.BlockSpec(memory_space=pl.ANY),
            pl.BlockSpec(memory_space=pltpu.VMEM),
        ],
        out_specs=[pl.BlockSpec(memory_space=pltpu.VMEM)] * 4,
        out_shape=[
            jax.ShapeDtypeStruct((SLOTS, 128), F32),
            jax.ShapeDtypeStruct((SLOTS, D), F32),
            jax.ShapeDtypeStruct((2, nq, D), BF),
            jax.ShapeDtypeStruct((D // 4, D), F32),
        ],
        scratch_shapes=[pltpu.VMEM((2 * nq, PAY), BF), pltpu.VMEM((D, D), F32), pltpu.SemaphoreType.DMA],
        compiler_params=pltpu.CompilerParams(vmem_limit_bytes=60 * 2**20),
        name="loss",
    )(place, buf, proj)


def split(v):
    hi = v.astype(BF)
    return hi, (v - hi.astype(F32)).astype(BF)


def dot(a, b):
    return jnp.dot(a, b, preferred_element_type=F32)


def dot_nt(a, b):
    return lax.dot_general(a, b, NT, preferred_element_type=F32)


def dot_tn(a, b):
    return lax.dot_general(a, b, TN, preferred_element_type=F32)


def norm(x, gain):
    inv = lax.rsqrt(jnp.mean(x * x, axis=-1, keepdims=True) + EPSILON)
    scaled = x * inv
    return inv, scaled, (scaled * gain).astype(BF)


def norm_back(g, inv, scaled, gain):
    gs = g * gain
    return inv * (gs - scaled * jnp.mean(gs * scaled, axis=-1, keepdims=True)), jnp.sum(g * scaled, axis=0)


def local(
    tokens_in,
    query_lengths,
    positive_ids,
    gain_attn,
    gain_ffn,
    w_query,
    w_key,
    w_value,
    w_out,
    rel_bias,
    w_in,
    w_ffn_out,
    w_proj,
):
    f = lax.axis_index("fsdp")
    t = lax.axis_index("tower")
    z = lax.axis_index("dp")
    n_dp = lax.axis_size("dp")
    rows = n_dp * 4
    is_query = t == 0
    small = jnp.concatenate(
        [gain_attn, gain_ffn, rel_bias.reshape(-1), jnp.zeros((32,), F32)]
    ).astype(BF)
    small = lax.all_gather(small, "fsdp", axis=0)
    gain_one = small[:, :192].reshape(1, D).astype(F32)
    gain_two = small[:, 192:384].reshape(1, D).astype(F32)
    table = small[:, 384 : 384 + 96].reshape(NB, H)
    w_qkv = gather_group(jnp.concatenate([w_query, w_key, w_value], axis=1).astype(BF))
    w_mid = gather_group(jnp.concatenate([w_out, w_in], axis=1).astype(BF))
    w_o, w_i = w_mid[:, :D], w_mid[:, D:]
    w_f = gather_group(w_ffn_out.astype(BF))
    w_p = gather_group(w_proj.astype(BF))

    lengths = query_lengths[:, 0]
    ends = jnp.cumsum(lengths, axis=-1)
    places = lax.broadcasted_iota(jnp.int32, (MB, SEQ, QSEG), 1)
    segment = jnp.where(is_query, jnp.sum((places >= ends[:, None, :]).astype(jnp.int32), axis=-1), 0)
    slot_ids = lax.broadcasted_iota(jnp.int32, (MB, QSEG), 1)
    counts = jnp.where(is_query, lengths, jnp.where(slot_ids < 1, SEQ, 0))
    seg = segment.reshape(T)
    lane = lax.broadcasted_iota(jnp.int32, (T, 128), 1) % 64
    hot_seg = lane == seg[:, None]
    fq = jnp.where(hot_seg, 1.0, 0.0).astype(BF)
    fk = jnp.where((lane < QSEG) & ~hot_seg, -1e30, 0.0).astype(BF)
    slot_of = seg + QSEG * (lax.broadcasted_iota(jnp.int32, (T,), 0) // SEQ)
    member = (slot_of[:, None] == lax.broadcasted_iota(jnp.int32, (T, SLOTS), 1)).astype(BF)
    member_t = (slot_of[None, :] == lax.broadcasted_iota(jnp.int32, (SLOTS, T), 0)).astype(BF)
    bias = bias_blocks(jnp.pad(table.T, ((0, 4), (0, 0))), diag_hot())

    x = tokens_in.reshape(T, D).astype(F32)
    inv1, r1, n1 = norm(x, gain_one)
    qkv = dot(n1, w_qkv).astype(BF)
    o, ot, e, li = attn_fwd(qkv, fq, fk, bias)
    x2 = x + dot(o, w_o)
    inv2, r2, n2 = norm(x2, gain_two)
    u = dot(n2, w_i)
    th = jnp.tanh(GELU_C * (u + 0.044715 * u * u * u))
    hh = (0.5 * u * (1.0 + th)).astype(BF)
    gp = (0.5 * (1.0 + th) + 0.5 * u * (1.0 - th * th) * (GELU_C * (1.0 + 3 * 0.044715 * u * u))).astype(BF)
    acts = dot(member_t, hh)
    x2_hi, x2_lo = split(x2)
    acts_hi, acts_lo = split(acts)
    count = jnp.maximum(counts, 1).astype(F32).reshape(SLOTS, 1)
    pooled = (dot(member_t, x2_hi) + dot(member_t, x2_lo) + dot(acts_hi, w_f) + dot(acts_lo, w_f)) / count
    info = jnp.concatenate(
        [
            counts.reshape(SLOTS, 1).astype(F32),
            positive_ids.reshape(SLOTS, 1).astype(F32),
            jnp.zeros((SLOTS, 126), F32),
        ],
        axis=1,
    )
    buf = jnp.concatenate([pooled, info], axis=1).astype(BF)
    buf = jnp.concatenate([buf, swap(buf, "fsdp", 1)], axis=0)
    buf = jnp.concatenate([buf, swap(buf, "fsdp", 2)], axis=0)
    buf = jnp.concatenate([buf, swap(buf, "tower", 1)], axis=0)
    bit = 1
    while bit < n_dp:
        buf = jnp.concatenate([buf, swap(buf, "dp", bit)], axis=0)
        bit *= 2
    place = jnp.stack([z * 8 + t * 4 + f, is_query.astype(jnp.int32), z * 4 + f, f]).astype(jnp.int32)
    loss, own, gf_all, grad_proj = loss_call(place, buf, w_p, rows)
    query_loss = loss[:, 0].reshape(MB, 1, QSEG)
    acts_all = lax.all_gather(acts_hi, ALL, axis=0, tiled=True)
    acts_mine = lax.dynamic_slice_in_dim(acts_all, f * D, D, 1)
    grad_ffn_out = dot_tn(acts_mine, gf_all.reshape(2 * rows * SLOTS, D))

    gf = own.astype(BF)
    gh_hi, gh_lo = split(dot_nt(gf, w_f))
    own_hi, own_lo = split(own)
    g_x3 = dot(member, own_hi) + dot(member, own_lo)
    gu = ((dot(member, gh_hi) + dot(member, gh_lo)) * gp.astype(F32)).astype(BF)
    grad_in = dot_tn(n2, gu)
    g_n2 = dot_nt(gu, w_i)
    back2, grad_gain_two = norm_back(g_n2, inv2, r2, gain_two)
    g_x2 = g_x3 + back2
    ga = g_x2.astype(BF)
    grad_out = dot(ot, ga)
    go = dot_nt(ga, w_o).astype(BF)
    dq, dk, dv, diag = attn_bwd(qkv, go, ot, e, li)
    dqkv = jnp.concatenate([dq, dk, dv], axis=1)
    grad_qkv = dot_tn(n1, dqkv)
    g_n1 = dot_nt(dqkv, w_qkv)
    back1, grad_gain_one = norm_back(g_n1, inv1, r1, gain_one)
    grad_tokens = (g_x2 + back1).astype(BF).reshape(1, MB, 1, SEQ, D)
    grad_table = jnp.einsum("hc,cb->bh", diag.reshape(H, 8192), diag_hot2(), precision=HIGHEST)

    mid = reduce_group(jnp.concatenate([grad_out, grad_in], axis=1).astype(BF))
    first = reduce_group(grad_qkv.astype(BF))
    tiny = jnp.concatenate([grad_gain_one, grad_gain_two, grad_table.reshape(-1)])
    tiny = lax.psum(tiny, ALL)
    return (
        query_loss,
        grad_tokens,
        lax.dynamic_slice_in_dim(tiny[:D], f * 192, 192, 0),
        lax.dynamic_slice_in_dim(tiny[D : 2 * D], f * 192, 192, 0),
        first[:, :D],
        first[:, D : 2 * D],
        first[:, 2 * D :],
        mid[:, :D],
        lax.dynamic_slice_in_dim(tiny[2 * D :].reshape(NB, H), f * 8, 8, 0),
        mid[:, D:],
        grad_ffn_out,
        grad_proj,
    )


def solution(mesh):
    rows = P(None, ("dp", "fsdp"), None)
    tokens = P("tower", None, ("dp", "fsdp"), None, None)
    vec, mat = P("fsdp"), P("fsdp", None)
    return jax.shard_map(
        local,
        mesh=mesh,
        in_specs=(tokens, rows, rows, vec, vec) + (mat,) * 8,
        out_specs=(rows, tokens, vec, vec) + (mat,) * 8,
        check_vma=False,
    )
```

time: 1110 us -> 475 us (0.43)
  waiting for transfers between devices: 604 us -> 138 us
  matrix products: 233 us -> 83 us
  Pallas kernels: 0 us -> 54.4 us
  local copies, waits for them, and re-layouts: 94.4 us -> 50 us
  blocking collectives: 87 us -> 62.4 us
  other arithmetic: 53 us -> 36.4 us
  starting transfers between devices: 13.5 us -> 28 us
    reduce_scatter x14 -> x0, waiting for transfers between devices: 305 us -> none  [the longest x2 98.9 us: reduce_now(): lax.psum_scatter(gradients[8].astype(jnp.bfloat16), 'fsdp', scatter_dimen...]
    psum x1 -> x0, waiting for transfers between devices: 164 us -> none  [reduce_now(): lax.psum((shards[0], shards[1], shards[2], shards[3], shards[4], shards[5...]
    dot_general x67 -> x21, matrix products: 233 us -> 83 us  [the longest x13 44.6 us: dot(): return jnp.dot(a, b, preferred_element_type=F32)]
    ppermute x4 -> x37, waiting for transfers between devices: 0.01 us -> 138 us  [swap(): return lax.ppermute(block, axis, [(i, i ^ bit) for i in range(size)])]
    unnamed x24 -> x1, waiting for transfers between devices: 84.8 us -> 0.02 us
    pallas_call x0 -> x4, Pallas kernels: none -> 54.4 us  [the longest x1 21.1 us: attn_bwd(): pl.pallas_call(attn_bwd_kernel, grid=(6, 2), in_specs=[pl.BlockSpec((SEQ,...]
    all_gather x7 -> x1, waiting for transfers between devices: 51 us -> 0.01 us  [local(): acts_all = lax.all_gather(acts_hi, ALL, axis=0, tiled=True)]
    convert_element_type x10 -> x3, local copies, waits for them, and re-layouts: 44.2 us -> 0.24 us  [the longest x1 0.09 us: local(): positive_ids.reshape(SLOTS, 1).astype(F32)]
  transfers between devices with their start and end apart: 27 -> 38, of which waited for: 13 -> 13; matrix products, arithmetic and copies ran while one was open for 30% -> 32% of each run, Pallas kernels for 0% -> 12%
where the time goes in v1:
time: 475 us; the launch traced here: 468 us
  waiting for transfers between devices  138 us (29%)
  matrix products  83 us (17%)
  blocking collectives  62.4 us (13%)
  Pallas kernels  54.4 us (11%)
  local copies, waits for them, and re-layouts  50 us (11%)
  other arithmetic  36.4 us (8%)
  starting transfers between devices  28 us (6%)
  between operations  15.4 us (3%)
    ppermute x37, waiting for transfers between devices, swap(): return lax.ppermute(block, axis, [(i, i ^ bit) for i in range(size)])  138 us
    psum x1, blocking collectives, local(): tiny = lax.psum(tiny, ALL)  46.2 us
    dot_general x13, matrix products, dot(): return jnp.dot(a, b, preferred_element_type=F32)  44.6 us
    ppermute x37, starting transfers between devices, swap(): return lax.ppermute(block, axis, [(i, i ^ bit) for i in range(size)])  28 us
    dot_general x4, matrix products, dot_nt(): return lax.dot_general(a, b, NT, preferred_element_type=F32)  23.7 us
    pallas_call x1, Pallas kernels, attn_bwd(): pl.pallas_call(attn_bwd_kernel, grid=(6, 2), in_specs=[pl.BlockSpec((SEQ,...  21.1 us
    pallas_call x1, Pallas kernels, attn_fwd(): pl.pallas_call(attn_fwd_kernel, grid=grid, in_specs=[pl.BlockSpec((SEQ, 1...  20.6 us
    dynamic_update_slice x20, local copies, waits for them, and re-layouts, gather_group(): full = lax.dynamic_update_slice_in_dim(full, piece, start, 0)  20.4 us
  transfers between devices with their start and end apart: 38, of which 13 were waited for; matrix products, arithmetic and copies ran while one was open for 32% of the time, Pallas kernels for 12%

profile of v1, /device:TPU:0, one launch (start us, length us, event | category | flops | bytes accessed | tf_op | source)
XLA Modules:
  0.0 468.1 jit_solution(11985668159995396012)
XLA Ops:
  26.8 3.4 constant_dynamic-update-slice_fusion.25
  32.8 16.2 %all-gather = bf16[4,1,512]{2,1,0:T(2,128)(2,1)S(1)} all-gather(bf16[1,1,512]{2,1,0:T(2,128)(2,1)S(1)} %fusion.130), channel_id=1, replica_groups=mesh['tower'=2,'dp'=4,'fsdp'=4] {'fsdp'}, dimensions={0}, use_global_device_ids=true | all-gather | bytes 5120 | tf_op jit(solution)/shard_map/all_gather | solution.py:358
  57.4 5.0 %bias_blocks.1.bias_ref = f32[12,7,128,128]{3,2,1,0:T(8,128)} custom-call(bf16[16,32]{1,0:T(8,128)(2,1)} %pad.4.tab_ref, bf16[32,1024]{1,0:T(8,128)(2,1)} %fusion.105.hot_ref), custom_call_target="tpu_custom_call" | custom-call | tf_op jit(solution)/shard_map/bias_blocks/pallas_call | solution.py:54
  71.0 6.4 %collective-permute-done.2 = bf16[96,2304]{1,0:T(8,128)(2,1)S(1)} collective-permute-done((bf16[96,2304]{1,0:T(8,128)(2,1)}, bf16[96,2304]{1,0:T(8,128)(2,1)S(1)}, u32[]{:S(2)}, u32[]{:S(2)}) %collective-permute-start.2) | collective-permute-done | bytes 442400 | tf_op jit(solution)/shard_map/ppermute | solution.py:164
  85.3 7.0 %collective-permute-done.12 = bf16[384,768]{1,0:T(8,128)(2,1)S(1)} collective-permute-done((bf16[384,768]{1,0:T(8,128)(2,1)}, bf16[384,768]{1,0:T(8,128)(2,1)S(1)}, u32[]{:S(2)}, u32[]{:S(2)}) %collective-permute-start.12) | collective-permute-done | bytes 589856 | tf_op jit(solution)/shard_map/ppermute | solution.py:164
  97.0 8.5 %convolution_convert_fusion.q_ref.k_ref.v_ref = bf16[1024,2304]{1,0:T(8,128)(2,1)} fusion(bf16[1024,768]{1,0:T(8,128)(2,1)S(1)} %fusion.18, bf16[768,2304]{1,0:T(8,128)(2,1)} %constant_dynamic-update-slice_fusion.32), kind=kOutput, calls=%fused_computation.18 | convolution fusion | flops 3626237952 | bytes 9830400 | tf_op jit(solution)/shard_map/dot_general | solution.py:312
  105.6 20.6 %attn_fwd.1 = (bf16[1024,768]{1,0:T(8,128)(2,1)S(1)}, bf16[768,1024]{1,0:T(8,128)(2,1)S(1)}, bf16[2,12,512,512]{3,2,1,0:T(8,128)(2,1)}, f32[2,12,8,512]{3,2,1,0:T(8,128)S(1)}) custom-call(bf16[1024,2304]{1,0:T(8,128)(2,1)} %convolution_convert_fusion.q_ref.k_ref.v_ref, bf16[1024,2304]{1,0:T(8,128)(2,1)} %convolution_convert_fusion.q_ref.k_ref.v_ref, ...), custom_call_target="tpu_custom_call" | custom-call | tf_op jit(solution)/shard_map/attn_fwd/pallas_call | solution.py:81
  133.1 5.1 %fusion.11 = f32[1024,3072]{1,0:T(8,128)S(1)} fusion(bf16[768,3840]{1,0:T(8,128)(2,1)S(1)} %constant_dynamic-update-slice_fusion.26, f32[1024,768]{1,0:T(8,128)S(1)} %get-tuple-element.120, f32[768]{0:T(1024)S(1)} %reshape.311, f32[1024]{0:T(1024)S(1)} %add_rsqrt_fusion), kind=kOutput, calls=%fused_computation.23 | convolution fusion | flops 4834197504 | bytes 20455424 | tf_op jit(solution)/shard_map/dot_general | solution.py:312
  138.2 5.1 %fusion.157 = (bf16[16,3072]{1,0:T(8,128)(2,1)S(1)}, f32[16,3072]{1,0:T(8,128)S(1)}) fusion(f32[1024,3072]{1,0:T(8,128)S(1)} %fusion.11, s32[1024]{0:T(1024)S(1)} %fusion.126), kind=kOutput, calls=%fused_computation.306 | convolution fusion | flops 129040384 | bytes 12881920 | tf_op jit(solution)/shard_map/dot_general | solution.py:312
  143.4 3.1 fusion.106
  146.5 3.1 fusion.37
  164.0 3.1 collective-permute-done.18
  167.8 2.7 collective-permute-start.19
  174.2 15.4 %collective-permute-done.19 = bf16[256,896]{1,0:T(8,128)(2,1)S(1)} collective-permute-done((bf16[256,896]{1,0:T(8,128)(2,1)}, bf16[256,896]{1,0:T(8,128)(2,1)S(1)}, u32[]{:S(2)}, u32[]{:S(2)}) %collective-permute-start.19) | collective-permute-done | bytes 458784 | tf_op jit(solution)/shard_map/ppermute | solution.py:164
  190.6 7.7 %loss.1 = (f32[16,128]{1,0:T(8,128)}, f32[16,768]{1,0:T(8,128)}, bf16[2,256,768]{2,1,0:T(8,128)(2,1)}, f32[192,768]{1,0:T(8,128)}) custom-call(s32[4]{0:T(128)} %pad_add_fusion.pos_ref, bf16[512,896]{1,0:T(8,128)(2,1)} %copy-done.17, bf16[768,768]{1,0:T(8,128)(2,1)} %constant_dynamic-update-slice_fusion.14.proj_ref), custom_call_target="tpu_custom_call" | custom-call | tf_op jit(solution)/shard_map/loss/pallas_call | solution.py:286
  198.2 3.7 fusion.133
  204.5 12.6 %multiply_convert_fusion = bf16[1024,3072]{1,0:T(8,128)(2,1)} fusion(f32[1024,3072]{1,0:T(8,128)S(1)} %fusion.83, f32[1024,3072]{1,0:T(8,128)} %copy-done.33, s32[1024]{0:T(1024)S(1)} %fusion.126, f32[16,3072]{1,0:T(8,128)S(1)} %fusion.133), kind=kOutput, calls=%fused_computation.9 | convolution fusion | flops 169934848 | bytes 31657984 | tf_op jit(solution)/shard_map/dot_general | solution.py:312
  217.1 8.2 %multiply_reduce_fusion = (f32[768]{0:T(1024)S(1)}, f32[1024]{0:T(1024)S(1)}, f32[1024,768]{1,0:T(8,128)S(1)}) fusion(f32[1024,768]{1,0:T(8,128)S(1)} %copy-done.3, f32[1024]{0:T(1024)S(1)} %add_rsqrt_fusion, f32[768]{0:T(1024)S(1)} %reshape.311, bf16[1024,3072]{1,0:T(8,128)(2,1)} %multiply_convert_fusion, bf16[768,3840]{1,0:T(8,128)(2,1)S(1)} %bitcast.111), kind=kOutput, calls=%fused_computation.42 | convolution fusion | flops 4836554752 | bytes 17316864 | tf_op jit(solution)/shard_map/dot_general | solution.py:316
  229.0 21.1 %attn_bwd.1 = (bf16[1024,768]{1,0:T(8,128)(2,1)S(1)}, bf16[1024,768]{1,0:T(8,128)(2,1)S(1)}, bf16[1024,768]{1,0:T(8,128)(2,1)S(1)}, f32[6,2,8,1024]{3,2,1,0:T(8,128)S(1)}) custom-call(bf16[1024,2304]{1,0:T(8,128)(2,1)} %convolution_convert_fusion.q_ref.k_ref.v_ref, bf16[1024,2304]{1,0:T(8,128)(2,1)} %convolution_convert_fusion.q_ref.k_ref.v_ref, ...), custom_call_target="tpu_custom_call" | custom-call | tf_op jit(solution)/shard_map/attn_bwd/pallas_call | solution.py:152
  251.7 4.1 convolution_convert_fusion.2
  257.7 5.9 %convolution_convert_fusion.1 = bf16[768,3072]{1,0:T(8,128)(2,1)S(1)} fusion(bf16[1024,3072]{1,0:T(8,128)(2,1)S(1)} %bitcast.136, f32[1024,768]{1,0:T(8,128)S(1)} %copy-done.3, f32[768]{0:T(1024)S(1)} %reshape.311, f32[1024]{0:T(1024)S(1)} %add_rsqrt_fusion), kind=kOutput, calls=%fused_computation.19 | convolution fusion | flops 4836556800 | bytes 14162944 | tf_op jit(solution)/shard_map/dot_general | solution.py:320
  274.7 9.2 %fusion.24 = (f32[768]{0:T(1024)S(1)}, f32[1024]{0:T(1024)S(1)}, f32[1024,768]{1,0:T(8,128)}) fusion(bf16[1,2,1,512,768]{4,3,2,1,0:T(8,128)(2,1)S(1)} %copy-done.5, f32[1024]{0:T(1024)S(1)} %bitcast.125, f32[768]{0:T(1024)S(1)} %reshape.310, bf16[1024,2304]{1,0:T(8,128)(2,1)} %copy-done.23, bf16[768,2304]{1,0:T(8,128)(2,1)} %constant_dynamic-update-slice_fusion.32), kind=kOutput, calls=%fused_computation.40 | convolution fusion | flops 3629381888 | bytes 12990464 | tf_op jit(solution)/shard_map/dot_general | solution.py:316
  283.9 46.2 %psum.7 = f32[1920]{0:T(1024)S(1)} all-reduce(f32[1920]{0:T(1024)S(1)} %pad_maximum_fusion.7), channel_id=1, replica_groups=mesh['tower'=2,'dp'=4,'fsdp'=4] {'tower','dp','fsdp'}, use_global_device_ids=true, to_apply=%region_8.9 | all-reduce | flops 1920 | bytes 15360 | tf_op jit(solution)/shard_map/psum | solution.py:445
  331.6 3.4 fusion.8
  340.0 7.3 %collective-permute-done.27 = bf16[96,2304]{1,0:T(8,128)(2,1)S(1)} collective-permute-done((bf16[96,2304]{1,0:T(8,128)(2,1)S(1)}, bf16[96,2304]{1,0:T(8,128)(2,1)S(1)}, u32[]{:S(2)}, u32[]{:S(2)}) %collective-permute-start.27) | collective-permute-done | bytes 442400 | tf_op jit(solution)/shard_map/ppermute | solution.py:164
  347.5 20.9 %collective-permute-done.32 = bf16[192,3840]{1,0:T(8,128)(2,1)S(1)} collective-permute-done((bf16[192,3840]{1,0:T(8,128)(2,1)S(1)}, bf16[192,3840]{1,0:T(8,128)(2,1)S(1)}, u32[]{:S(2)}, u32[]{:S(2)}) %collective-permute-start.32) | collective-permute-done | bytes 1474592 | tf_op jit(solution)/shard_map/ppermute | solution.py:164
  370.3 14.8 %collective-permute-done.33 = bf16[96,3840]{1,0:T(8,128)(2,1)S(1)} collective-permute-done((bf16[96,3840]{1,0:T(8,128)(2,1)S(1)}, bf16[96,3840]{1,0:T(8,128)(2,1)S(1)}, u32[]{:S(2)}, u32[]{:S(2)}) %collective-permute-start.33) | collective-permute-done | bytes 737312 | tf_op jit(solution)/shard_map/ppermute | solution.py:164
  385.6 3.8 collective-permute-done.29
  391.9 13.1 %collective-permute-done.34 = bf16[96,3840]{1,0:T(8,128)(2,1)S(1)} collective-permute-done((bf16[96,3840]{1,0:T(8,128)(2,1)S(1)}, bf16[96,3840]{1,0:T(8,128)(2,1)S(1)}, u32[]{:S(2)}, u32[]{:S(2)}) %collective-permute-start.34) | collective-permute-done | bytes 737312 | tf_op jit(solution)/shard_map/ppermute | solution.py:164
  408.8 30.7 %collective-permute-done.35 = bf16[96,3840]{1,0:T(8,128)(2,1)S(1)} collective-permute-done((bf16[96,3840]{1,0:T(8,128)(2,1)S(1)}, bf16[96,3840]{1,0:T(8,128)(2,1)S(1)}, u32[]{:S(2)}, u32[]{:S(2)}) %collective-permute-start.35) | collective-permute-done | bytes 737312 | tf_op jit(solution)/shard_map/ppermute | solution.py:164
  442.4 3.3 fusion.54
  445.8 12.4 %collective-permute-done.36 = bf16[96,3840]{1,0:T(8,128)(2,1)S(1)} collective-permute-done((bf16[96,3840]{1,0:T(8,128)(2,1)S(1)}, bf16[96,3840]{1,0:T(8,128)(2,1)S(1)}, u32[]{:S(2)}, u32[]{:S(2)}) %collective-permute-start.36) | collective-permute-done | bytes 737312 | tf_op jit(solution)/shard_map/ppermute | solution.py:164
  (293 shorter events, 119.6 us)
Async XLA Ops:
  7.2 435.2 %all-gather.3.cloned.1.call-start = ((), (), s32[]{:S(2)}) async-start(), calls=%async_computation | async-start | bytes 3244032 | tf_op jit(solution)/shard_map/all_gather | solution.py:418
  13.6 52.7 %collective-permute-start = (bf16[192,2304]{1,0:T(8,128)(2,1)S(1)}, bf16[192,2304]{1,0:T(8,128)(2,1)}, u32[]{:S(2)}, u32[]{:S(2)}) collective-permute-start(bf16[192,2304]{1,0:T(8,128)(2,1)S(1)} %get-tuple-element.103), channel_id=1, source_target_pairs={{0,1},{1,0},{2,3},{3,2},{4,5},{5,4},{6,7},{7,6},{8,9},{9,8},{10,11... | collective-permute-start | bytes 2654216 | tf_op jit(solution)/shard_map/ppermute | solution.py:164
  14.9 49.9 %collective-permute-start.1 = (bf16[96,2304]{1,0:T(8,128)(2,1)}, bf16[96,2304]{1,0:T(8,128)(2,1)}, u32[]{:S(2)}, u32[]{:S(2)}) collective-permute-start(bf16[96,2304]{1,0:T(8,128)(2,1)} %constant_dynamic-slice_fusion.3), channel_id=1, source_target_pairs={{0,2},{1,3},{2,0},{3,1},{4,6},{5,7},{6,4},{7,5},{8,10},{9,11},{10,... | collective-permute-start | bytes 1327112 | tf_op jit(solution)/shard_map/ppermute | solution.py:164
  24.0 102.2 %collective-permute-start.5 = (bf16[192,3840]{1,0:T(8,128)(2,1)}, bf16[192,3840]{1,0:T(8,128)(2,1)}, u32[]{:S(2)}, u32[]{:S(2)}) collective-permute-start(bf16[192,3840]{1,0:T(8,128)(2,1)} %get-tuple-element.99), channel_id=1, source_target_pairs={{0,1},{1,0},{2,3},{3,2},{4,5},{5,4},{6,7},{7,6},{8,9},{9,8},{10,11... | collective-permute-start | bytes 4423688 | tf_op jit(solution)/shard_map/ppermute | solution.py:164
  30.2 50.4 %collective-permute-start.10 = (bf16[768,768]{1,0:T(8,128)(2,1)}, bf16[768,768]{1,0:T(8,128)(2,1)}, u32[]{:S(2)}, u32[]{:S(2)}) collective-permute-start(bf16[768,768]{1,0:T(8,128)(2,1)} %get-tuple-element.93), channel_id=1, source_target_pairs={{0,1},{1,0},{2,3},{3,2},{4,5},{5,4},{6,7},{7,6},{8,9},{9,8},{10,11... | collective-permute-start | bytes 3538952 | tf_op jit(solution)/shard_map/ppermute | solution.py:164
  32.3 38.0 %collective-permute-start.11 = (bf16[384,768]{1,0:T(8,128)(2,1)}, bf16[384,768]{1,0:T(8,128)(2,1)}, u32[]{:S(2)}, u32[]{:S(2)}) collective-permute-start(bf16[384,768]{1,0:T(8,128)(2,1)} %constant_dynamic-slice_fusion.2), channel_id=1, source_target_pairs={{0,2},{1,3},{2,0},{3,1},{4,6},{5,7},{6,4},{7,5},{8,10},{9,11},{10,... | collective-permute-start | bytes 1769480 | tf_op jit(solution)/shard_map/ppermute | solution.py:164
  64.7 12.7 %collective-permute-start.2 = (bf16[96,2304]{1,0:T(8,128)(2,1)}, bf16[96,2304]{1,0:T(8,128)(2,1)S(1)}, u32[]{:S(2)}, u32[]{:S(2)}) collective-permute-start(bf16[96,2304]{1,0:T(8,128)(2,1)} %collective-permute-done.1), channel_id=1, source_target_pairs={{0,16},{16,0},{1,17},{17,1},{2,18},{18,2},{3,19},{19,3},{4,20},{20... | collective-permute-start | bytes 1327112 | tf_op jit(solution)/shard_map/ppermute | solution.py:164
  66.3 13.4 %collective-permute-start.3 = (bf16[96,2304]{1,0:T(8,128)(2,1)}, bf16[96,2304]{1,0:T(8,128)(2,1)S(1)}, u32[]{:S(2)}, u32[]{:S(2)}) collective-permute-start(bf16[96,2304]{1,0:T(8,128)(2,1)} %collective-permute-done.1), channel_id=1, source_target_pairs={{0,1},{1,0},{2,3},{3,2},{4,5},{5,4},{6,7},{7,6},{8,9},{9,8},{10,11... | collective-permute-start | bytes 1327112 | tf_op jit(solution)/shard_map/ppermute | solution.py:164
  70.4 22.9 %collective-permute-start.6 = (bf16[96,3840]{1,0:T(8,128)(2,1)S(1)}, bf16[96,3840]{1,0:T(8,128)(2,1)S(1)}, u32[]{:S(2)}, u32[]{:S(2)}) collective-permute-start(bf16[96,3840]{1,0:T(8,128)(2,1)S(1)} %fusion.60), channel_id=1, source_target_pairs={{0,2},{1,3},{2,0},{3,1},{4,6},{5,7},{6,4},{7,5},{8,10},{9,11},{10,... | collective-permute-start | bytes 2211848 | tf_op jit(solution)/shard_map/ppermute | solution.py:164
  77.4 15.0 %collective-permute-start.12 = (bf16[384,768]{1,0:T(8,128)(2,1)}, bf16[384,768]{1,0:T(8,128)(2,1)S(1)}, u32[]{:S(2)}, u32[]{:S(2)}) collective-permute-start(bf16[384,768]{1,0:T(8,128)(2,1)} %collective-permute-done.11), channel_id=1, source_target_pairs={{0,16},{16,0},{1,17},{17,1},{2,18},{18,2},{3,19},{19,3},{4,20},{20... | collective-permute-start | bytes 1769480 | tf_op jit(solution)/shard_map/ppermute | solution.py:164
  79.7 14.0 %collective-permute-start.13 = (bf16[384,768]{1,0:T(8,128)(2,1)}, bf16[384,768]{1,0:T(8,128)(2,1)S(1)}, u32[]{:S(2)}, u32[]{:S(2)}) collective-permute-start(bf16[384,768]{1,0:T(8,128)(2,1)} %collective-permute-done.11), channel_id=1, source_target_pairs={{0,1},{1,0},{2,3},{3,2},{4,5},{5,4},{6,7},{7,6},{8,9},{9,8},{10,11... | collective-permute-start | bytes 1769480 | tf_op jit(solution)/shard_map/ppermute | solution.py:164
  80.5 15.7 %collective-permute-start.4 = (bf16[96,2304]{1,0:T(8,128)(2,1)S(1)}, bf16[96,2304]{1,0:T(8,128)(2,1)S(1)}, u32[]{:S(2)}, u32[]{:S(2)}) collective-permute-start(bf16[96,2304]{1,0:T(8,128)(2,1)S(1)} %collective-permute-done.2), channel_id=1, source_target_pairs={{0,1},{1,0},{2,3},{3,2},{4,5},{5,4},{6,7},{7,6},{8,9},{9,8},{10,11... | collective-permute-start | bytes 1327112 | tf_op jit(solution)/shard_map/ppermute | solution.py:164
  92.4 60.9 %collective-permute-start.20 = (bf16[192,768]{1,0:T(8,128)(2,1)S(1)}, bf16[192,768]{1,0:T(8,128)(2,1)}, u32[]{:S(2)}, u32[]{:S(2)}) collective-permute-start(bf16[192,768]{1,0:T(8,128)(2,1)S(1)} %copy-done.21), channel_id=1, source_target_pairs={{0,1},{1,0},{2,3},{3,2},{4,5},{5,4},{6,7},{7,6},{8,9},{9,8},{10,11... | collective-permute-start | bytes 884744 | tf_op jit(solution)/shard_map/ppermute | solution.py:164
  93.3 58.0 %collective-permute-start.21 = (bf16[96,768]{1,0:T(8,128)(2,1)}, bf16[96,768]{1,0:T(8,128)(2,1)}, u32[]{:S(2)}, u32[]{:S(2)}) collective-permute-start(bf16[96,768]{1,0:T(8,128)(2,1)} %constant_dynamic-slice_fusion.1), channel_id=1, source_target_pairs={{0,2},{1,3},{2,0},{3,1},{4,6},{5,7},{6,4},{7,5},{8,10},{9,11},{10,... | collective-permute-start | bytes 442376 | tf_op jit(solution)/shard_map/ppermute | solution.py:164
  93.7 33.0 %collective-permute-start.7 = (bf16[96,3840]{1,0:T(8,128)(2,1)S(1)}, bf16[96,3840]{1,0:T(8,128)(2,1)S(1)}, u32[]{:S(2)}, u32[]{:S(2)}) collective-permute-start(bf16[96,3840]{1,0:T(8,128)(2,1)S(1)} %collective-permute-done.6), channel_id=1, source_target_pairs={{0,16},{16,0},{1,17},{17,1},{2,18},{18,2},{3,19},{19,3},{4,20},{20... | collective-permute-start | bytes 2211848 | tf_op jit(solution)/shard_map/ppermute | solution.py:164
  96.2 32.3 %collective-permute-start.8 = (bf16[96,3840]{1,0:T(8,128)(2,1)S(1)}, bf16[96,3840]{1,0:T(8,128)(2,1)S(1)}, u32[]{:S(2)}, u32[]{:S(2)}) collective-permute-start(bf16[96,3840]{1,0:T(8,128)(2,1)S(1)} %collective-permute-done.6), channel_id=1, source_target_pairs={{0,1},{1,0},{2,3},{3,2},{4,5},{5,4},{6,7},{7,6},{8,9},{9,8},{10,11... | collective-permute-start | bytes 2211848 | tf_op jit(solution)/shard_map/ppermute | solution.py:164
  151.3 20.8 %collective-permute-start.22 = (bf16[96,768]{1,0:T(8,128)(2,1)}, bf16[96,768]{1,0:T(8,128)(2,1)S(1)}, u32[]{:S(2)}, u32[]{:S(2)}) collective-permute-start(bf16[96,768]{1,0:T(8,128)(2,1)} %collective-permute-done.21), channel_id=1, source_target_pairs={{0,16},{16,0},{1,17},{17,1},{2,18},{18,2},{3,19},{19,3},{4,20},{20... | collective-permute-start | bytes 442376 | tf_op jit(solution)/shard_map/ppermute | solution.py:164
  151.6 21.2 %collective-permute-start.23 = (bf16[96,768]{1,0:T(8,128)(2,1)}, bf16[96,768]{1,0:T(8,128)(2,1)S(1)}, u32[]{:S(2)}, u32[]{:S(2)}) collective-permute-start(bf16[96,768]{1,0:T(8,128)(2,1)} %collective-permute-done.21), channel_id=1, source_target_pairs={{0,1},{1,0},{2,3},{3,2},{4,5},{5,4},{6,7},{7,6},{8,9},{9,8},{10,11... | collective-permute-start | bytes 442376 | tf_op jit(solution)/shard_map/ppermute | solution.py:164
  161.0 6.1 %collective-permute-start.18 = (bf16[128,896]{1,0:T(8,128)(2,1)S(1)}, bf16[128,896]{1,0:T(8,128)(2,1)S(1)}, u32[]{:S(2)}, u32[]{:S(2)}) collective-permute-start(bf16[128,896]{1,0:T(8,128)(2,1)S(1)} %pad_maximum_fusion.3), channel_id=1, source_target_pairs={{0,4},{4,0},{8,12},{12,8},{1,5},{5,1},{9,13},{13,9},{2,6},{6,2},{1... | collective-permute-start | bytes 688136 | tf_op jit(solution)/shard_map/ppermute | solution.py:164
  167.8 21.7 %collective-permute-start.19 = (bf16[256,896]{1,0:T(8,128)(2,1)}, bf16[256,896]{1,0:T(8,128)(2,1)S(1)}, u32[]{:S(2)}, u32[]{:S(2)}) collective-permute-start(bf16[256,896]{1,0:T(8,128)(2,1)} %get-tuple-element.105), channel_id=1, source_target_pairs={{0,8},{4,12},{8,0},{12,4},{1,9},{5,13},{9,1},{13,5},{2,10},{6,14},... | collective-permute-start | bytes 1376264 | tf_op jit(solution)/shard_map/ppermute | solution.py:164
  257.7 12.2 %collective-permute-start.25 = (bf16[2,192,2304]{2,1,0:T(8,128)(2,1)S(1)}, bf16[2,192,2304]{2,1,0:T(8,128)(2,1)}, u32[]{:S(2)}, u32[]{:S(2)}) collective-permute-start(bf16[2,192,2304]{2,1,0:T(8,128)(2,1)S(1)} %dynamic-slice_bitcast_fusion), channel_id=1, source_target_pairs={{0,1},{1,0},{2,3},{3,2},{4,5},{5,4},{6,7},{7,6},{8,9},{9,8},{10,11... | collective-permute-start | bytes 5308424 | tf_op jit(solution)/shard_map/ppermute | solution.py:164
  267.6 63.9 %collective-permute-start.31 = (bf16[2,192,3840]{2,1,0:T(8,128)(2,1)}, bf16[2,192,3840]{2,1,0:T(8,128)(2,1)}, u32[]{:S(2)}, u32[]{:S(2)}) collective-permute-start(bf16[2,192,3840]{2,1,0:T(8,128)(2,1)} %fusion.27), channel_id=1, source_target_pairs={{0,1},{1,0},{2,3},{3,2},{4,5},{5,4},{6,7},{7,6},{8,9},{9,8},{10,11... | collective-permute-start | bytes 8847368 | tf_op jit(solution)/shard_map/ppermute | solution.py:164
  273.3 56.7 %collective-permute-start.26 = (bf16[192,2304]{1,0:T(8,128)(2,1)}, bf16[192,2304]{1,0:T(8,128)(2,1)}, u32[]{:S(2)}, u32[]{:S(2)}) collective-permute-start(bf16[192,2304]{1,0:T(8,128)(2,1)} %dynamic-slice_bitcast_fusion.2), channel_id=1, source_target_pairs={{0,2},{1,3},{2,0},{3,1},{4,6},{5,7},{6,4},{7,5},{8,10},{9,11},{10,... | collective-permute-start | bytes 2654216 | tf_op jit(solution)/shard_map/ppermute | solution.py:164
  335.1 33.3 %collective-permute-start.32 = (bf16[192,3840]{1,0:T(8,128)(2,1)S(1)}, bf16[192,3840]{1,0:T(8,128)(2,1)S(1)}, u32[]{:S(2)}, u32[]{:S(2)}) collective-permute-start(bf16[192,3840]{1,0:T(8,128)(2,1)S(1)} %dynamic-slice_bitcast_fusion.1), channel_id=1, source_target_pairs={{0,2},{1,3},{2,0},{3,1},{4,6},{5,7},{6,4},{7,5},{8,10},{9,11},{10,... | collective-permute-start | bytes 4423688 | tf_op jit(solution)/shard_map/ppermute | solution.py:164
  337.5 9.8 %collective-permute-start.27 = (bf16[96,2304]{1,0:T(8,128)(2,1)S(1)}, bf16[96,2304]{1,0:T(8,128)(2,1)S(1)}, u32[]{:S(2)}, u32[]{:S(2)}) collective-permute-start(bf16[96,2304]{1,0:T(8,128)(2,1)S(1)} %dynamic-slice_bitcast_fusion.4), channel_id=1, source_target_pairs={{0,16},{16,0},{1,17},{17,1},{2,18},{18,2},{3,19},{19,3},{4,20},{20... | collective-permute-start | bytes 1327112 | tf_op jit(solution)/shard_map/ppermute | solution.py:164
  347.4 22.7 %collective-permute-start.28 = (bf16[96,2304]{1,0:T(8,128)(2,1)S(1)}, bf16[96,2304]{1,0:T(8,128)(2,1)S(1)}, u32[]{:S(2)}, u32[]{:S(2)}) collective-permute-start(bf16[96,2304]{1,0:T(8,128)(2,1)S(1)} %fusion.53), channel_id=1, source_target_pairs={{0,4},{4,0},{8,12},{12,8},{1,5},{5,1},{9,13},{13,9},{2,6},{6,2},{1... | collective-permute-start | bytes 1327112 | tf_op jit(solution)/shard_map/ppermute | solution.py:164
  368.8 16.3 %collective-permute-start.33 = (bf16[96,3840]{1,0:T(8,128)(2,1)S(1)}, bf16[96,3840]{1,0:T(8,128)(2,1)S(1)}, u32[]{:S(2)}, u32[]{:S(2)}) collective-permute-start(bf16[96,3840]{1,0:T(8,128)(2,1)S(1)} %dynamic-slice_bitcast_fusion.3), channel_id=1, source_target_pairs={{0,16},{16,0},{1,17},{17,1},{2,18},{18,2},{3,19},{19,3},{4,20},{20... | collective-permute-start | bytes 2211848 | tf_op jit(solution)/shard_map/ppermute | solution.py:164
  370.2 19.1 %collective-permute-start.29 = (bf16[96,2304]{1,0:T(8,128)(2,1)S(1)}, bf16[96,2304]{1,0:T(8,128)(2,1)}, u32[]{:S(2)}, u32[]{:S(2)}) collective-permute-start(bf16[96,2304]{1,0:T(8,128)(2,1)S(1)} %add_convert_fusion.3), channel_id=1, source_target_pairs={{0,8},{4,12},{8,0},{12,4},{1,9},{5,13},{9,1},{13,5},{2,10},{6,14},... | collective-permute-start | bytes 1327112 | tf_op jit(solution)/shard_map/ppermute | solution.py:164
  385.3 19.7 %collective-permute-start.34 = (bf16[96,3840]{1,0:T(8,128)(2,1)S(1)}, bf16[96,3840]{1,0:T(8,128)(2,1)S(1)}, u32[]{:S(2)}, u32[]{:S(2)}) collective-permute-start(bf16[96,3840]{1,0:T(8,128)(2,1)S(1)} %fusion.33), channel_id=1, source_target_pairs={{0,4},{4,0},{8,12},{12,8},{1,5},{5,1},{9,13},{13,9},{2,6},{6,2},{1... | collective-permute-start | bytes 2211848 | tf_op jit(solution)/shard_map/ppermute | solution.py:164
  390.5 17.2 %collective-permute-start.30 = (bf16[96,2304]{1,0:T(8,128)(2,1)S(1)}, bf16[96,2304]{1,0:T(8,128)(2,1)}, u32[]{:S(2)}, u32[]{:S(2)}) collective-permute-start(bf16[96,2304]{1,0:T(8,128)(2,1)S(1)} %add_convert_fusion.2), channel_id=1, source_target_pairs={{0,16},{16,0},{1,17},{17,1},{2,18},{18,2},{3,19},{19,3},{4,20},{20... | collective-permute-start | bytes 1327112 | tf_op jit(solution)/shard_map/ppermute | solution.py:164
  405.1 34.4 %collective-permute-start.35 = (bf16[96,3840]{1,0:T(8,128)(2,1)S(1)}, bf16[96,3840]{1,0:T(8,128)(2,1)S(1)}, u32[]{:S(2)}, u32[]{:S(2)}) collective-permute-start(bf16[96,3840]{1,0:T(8,128)(2,1)S(1)} %add_convert_fusion.1), channel_id=1, source_target_pairs={{0,8},{4,12},{8,0},{12,4},{1,9},{5,13},{9,1},{13,5},{2,10},{6,14},... | collective-permute-start | bytes 2211848 | tf_op jit(solution)/shard_map/ppermute | solution.py:164
  439.7 18.5 %collective-permute-start.36 = (bf16[96,3840]{1,0:T(8,128)(2,1)S(1)}, bf16[96,3840]{1,0:T(8,128)(2,1)S(1)}, u32[]{:S(2)}, u32[]{:S(2)}) collective-permute-start(bf16[96,3840]{1,0:T(8,128)(2,1)S(1)} %add_convert_fusion), channel_id=1, source_target_pairs={{0,16},{16,0},{1,17},{17,1},{2,18},{18,2},{3,19},{19,3},{4,20},{20... | collective-permute-start | bytes 2211848 | tf_op jit(solution)/shard_map/ppermute | solution.py:164
  (46 other events, 407.1 us)
Sparse Core Ops, SparseCore 0:
  174.3 60.9 all-gather.2

commit v2 on v1

v2 whole, which is shorter than its diff:
```python
import functools

import jax
import jax.numpy as jnp
from jax import lax
from jax.experimental import pallas as pl
from jax.experimental.pallas import tpu as pltpu
from jax.sharding import PartitionSpec as P

D = 768
H = 12
DH = 64
FF = 3072
NB = 32
SEQ = 512
QSEG = 8
MB = 2
T = MB * SEQ
SLOTS = MB * QSEG
PAY = D + 128
FULL = PAY + 128
PAIRS = H // 2
PARTS = 3
PER = PAIRS // PARTS
EPSILON = 1e-06
LOGIT_SCALE = 50.0
LOSS_SCALE = 256.0
THRESHOLDS = (12, 16, 23, 32, 46, 64, 91)
GELU_C = 0.7978845608028654
ALL = ("tower", "dp", "fsdp")
BF = jnp.bfloat16
F32 = jnp.float32
HIGHEST = lax.Precision.HIGHEST
NT = (((1,), (1,)), ((), ()))
TN = (((0,), (0,)), ((), ()))


def bucket_of(m):
    a = jnp.abs(m)
    far = 8 + sum((a >= edge).astype(jnp.int32) for edge in THRESHOLDS)
    return jnp.where(m > 0, 16, 0) + jnp.where(a < 8, a, far)


def diag_hot():
    col = lax.broadcasted_iota(jnp.int32, (NB, 1024), 1)
    m = (col // 128 - 3) * 128 - col % 128
    return (bucket_of(m) == lax.broadcasted_iota(jnp.int32, (NB, 1024), 0)).astype(BF)


def diag_hot2():
    c = lax.broadcasted_iota(jnp.int32, (8192, NB), 0)
    s, col = c // 1024, c % 1024
    m = (col // 128 - 3) * 128 - (col % 128 - s) % 128
    return (bucket_of(m) == lax.broadcasted_iota(jnp.int32, (8192, NB), 1)).astype(F32)


def upper():
    return lax.broadcasted_iota(jnp.int32, (128, 128), 1) >= lax.broadcasted_iota(jnp.int32, (128, 128), 0)


def params(megabytes):
    return pltpu.CompilerParams(vmem_limit_bytes=megabytes * 2**20)


def cost(flops, moved):
    return pl.CostEstimate(flops=int(flops), bytes_accessed=int(moved), transcendentals=0)


SMEM = pl.BlockSpec(memory_space=pltpu.SMEM)
VMEM = pl.BlockSpec(memory_space=pltpu.VMEM)
HBM = pl.BlockSpec(memory_space=pltpu.HBM)


def sds(shape, kind):
    return jax.ShapeDtypeStruct(shape, kind)


def whole(shape):
    return pl.BlockSpec(shape, lambda *i: (0,) * len(shape))


def bias_kernel(tab_ref, hot_ref, out_ref):
    w = jnp.dot(tab_ref[...], hot_ref[...], preferred_element_type=F32)
    up = upper()
    for h in range(H):
        prev = None
        for e in range(8):
            row = jnp.broadcast_to(w[h : h + 1, e * 128 : (e + 1) * 128], (128, 128))
            r = pltpu.roll(row, 0, 1, stride=1, stride_axis=0)
            if e > 0:
                out_ref[h, e - 1] = jnp.where(up, prev, r)
            prev = r


def bias_blocks(table_t, hot):
    return pl.pallas_call(
        bias_kernel, out_shape=sds((H, 7, 128, 128), F32), cost_estimate=cost(5e9, 5e6), name="bias_blocks"
    )(table_t, hot)


def halves(pieces, f, t, stride, skip, size):
    own, mate, near, far, near_mate, far_mate = pieces
    table = (
        (own, skip, f, 0),
        (own, stride + skip, f, 1),
        (mate, skip, f ^ 1, 0),
        (mate, stride + skip, f ^ 1, 1),
        (near, skip, f ^ 2, t),
        (far, skip, f ^ 2, 1 - t),
        (near_mate, skip, f ^ 3, t),
        (far_mate, skip, f ^ 3, 1 - t),
    )
    return [(ref, start, pl.multiple_of((2 * q + h) * size, 32)) for ref, start, q, h in table]


def fetch(pieces, f, t, stride, skip, size, cols, dst, dst_cols, sem):
    for ref, start, to in halves(pieces, f, t, stride, skip, size):
        pltpu.make_async_copy(ref.at[pl.ds(start, size), cols], dst.at[pl.ds(to, size), dst_cols], sem).start()


def landed(ref, sem):
    pltpu.make_async_copy(ref, ref, sem).wait()


def norm(x, gain):
    inv = lax.rsqrt(jnp.mean(x * x, axis=-1, keepdims=True) + EPSILON)
    scaled = x * inv
    return inv, scaled, (scaled * gain).astype(BF)


def norm_back(g, inv, scaled, gain):
    gs = g * gain
    return inv * (gs - scaled * jnp.mean(gs * scaled, axis=-1, keepdims=True))


def norm_kernel(x_ref, gain_ref, n_ref, nt_ref):
    n = norm(x_ref[...].astype(F32), gain_ref[...])[2]
    n_ref[...] = n
    nt_ref[...] = n.T


def norm_call(x, gain):
    return pl.pallas_call(
        norm_kernel,
        grid=(2,),
        in_specs=[pl.BlockSpec((SEQ, D), lambda r: (r, 0)), whole((1, D))],
        out_specs=[pl.BlockSpec((SEQ, D), lambda r: (r, 0)), pl.BlockSpec((D, SEQ), lambda r: (0, r))],
        out_shape=[sds((T, D), BF), sds((D, T), BF)],
        compiler_params=params(40),
        cost_estimate=cost(2e9, 5e6),
        name="norm_attn",
    )(x, gain)


def qkv_kernel(place_ref, n_ref, *rest):
    pieces, out_ref, w, sems = rest[:6], rest[6], rest[7], rest[8]
    f, t = place_ref[0], place_ref[1]
    step = pl.program_id(0)

    @pl.when(step == 0)
    def _():
        for c in range(3):
            cols = pl.ds(c * D, D)
            fetch(pieces, f, t, 96, 0, 96, cols, w.at[c], pl.ds(0, D), sems.at[c])

    landed(w.at[step], sems.at[step])
    out_ref[...] = jnp.dot(n_ref[...], w[step], preferred_element_type=F32).astype(BF)


def qkv_call(place, n1, pieces):
    return pl.pallas_call(
        qkv_kernel,
        grid=(3,),
        in_specs=[SMEM, whole((T, D))] + [HBM] * 6,
        out_specs=pl.BlockSpec((T, D), lambda c: (0, c)),
        out_shape=sds((T, 3 * D), BF),
        scratch_shapes=[pltpu.VMEM((3, D, D), BF), pltpu.SemaphoreType.DMA((3,))],
        compiler_params=params(40),
        cost_estimate=cost(3.6e9, 1e7),
        name="qkv",
    )(place, n1, *pieces)


def attn_fwd_kernel(qkv_ref, fq_ref, fk_ref, bias_ref, o_ref, ot_ref, e_ref, li_ref):
    lane = lax.broadcasted_iota(jnp.int32, (SEQ, 128), 1)
    q, k = qkv_ref[:, :128], qkv_ref[:, 128:256]
    fq, fk = fq_ref[...], fk_ref[...]
    vt = qkv_ref[:, 256:].T
    outs = []
    for s in range(2):
        own = (lane < 64) if s == 0 else (lane >= 64)
        qa, ka = jnp.where(own, q, fq), jnp.where(own, k, fk)
        st = lax.dot_general(ka, qa, NT, preferred_element_type=F32)
        strips = [
            jnp.concatenate([bias_ref[s, bj - bi + 3] for bi in range(4)], axis=1) for bj in range(4)
        ]
        st = st + jnp.concatenate(strips, axis=0)
        top = jnp.max(st, axis=0, keepdims=True)
        e = jnp.exp(st - top).astype(BF)
        e_ref[0, s] = e
        va = jnp.concatenate([vt[64 * s : 64 * s + 64], jnp.ones((16, SEQ), BF)], axis=0)
        ot = jnp.dot(va, e, preferred_element_type=F32)
        linv = 1.0 / ot[64:65]
        li_ref[0, s] = jnp.broadcast_to(linv, (8, SEQ))
        outs.append((ot[:64] * linv).astype(BF))
    ot = jnp.concatenate(outs, axis=0)
    ot_ref[...] = ot
    o_ref[...] = ot.T


def attn_fwd(qkv, fq, fk, bias, first, count):
    return pl.pallas_call(
        attn_fwd_kernel,
        grid=(count, 2),
        in_specs=[
            pl.BlockSpec((SEQ, 384), lambda p, r: (r, first + p)),
            pl.BlockSpec((SEQ, 128), lambda p, r: (r, 0)),
            pl.BlockSpec((SEQ, 128), lambda p, r: (r, 0)),
            pl.BlockSpec((2, 7, 128, 128), lambda p, r: (first + p, 0, 0, 0)),
        ],
        out_specs=[
            pl.BlockSpec((SEQ, 128), lambda p, r: (r, p)),
            pl.BlockSpec((128, SEQ), lambda p, r: (p, r)),
            pl.BlockSpec((1, 2, SEQ, SEQ), lambda p, r: (r, p, 0, 0)),
            pl.BlockSpec((1, 2, 8, SEQ), lambda p, r: (r, p, 0, 0)),
        ],
        out_shape=[
            sds((T, 128 * count), BF),
            sds((128 * count, T), BF),
            sds((2, 2 * count, SEQ, SEQ), BF),
            sds((2, 2 * count, 8, SEQ), F32),
        ],
        compiler_params=params(40),
        cost_estimate=cost(3.3e9 * count, 3e6 * count),
        name="attn_fwd",
    )(qkv, fq, fk, bias)


def attn_bwd_kernel(
    place_ref, qkv_ref, do_ref, ot_ref, e_ref, li_ref, nt_ref, *rest
):
    d_ref, keep_ref, send_ref, diag_ref, acc, gacc = rest[-6:]
    r = pl.program_id(1)
    lane = lax.broadcasted_iota(jnp.int32, (SEQ, 128), 1)
    q, k, v = qkv_ref[:, :128], qkv_ref[:, 128:256], qkv_ref[:, 256:]
    do = do_ref[...]
    kt, dt = k.T, do.T
    dqs = []
    prod = dt.astype(F32) * ot_ref[...].astype(F32)
    for s in range(2):
        own = (lane < 64) if s == 0 else (lane >= 64)
        linv = li_ref[0, s, 0:1, :]
        delta = jnp.sum(prod[64 * s : 64 * s + 64], axis=0, keepdims=True)
        vm = jnp.where(own, v, jnp.zeros_like(v))
        dp = lax.dot_general(vm, do, NT, preferred_element_type=F32)
        p = e_ref[0, s].astype(F32) * linv
        ds32 = p * (dp - delta)
        ds = ds32.astype(BF)
        dvh = jnp.dot(p.astype(BF), do, preferred_element_type=F32)
        dkh = jnp.dot(ds, q, preferred_element_type=F32)
        dqs.append(jnp.dot(kt[64 * s : 64 * s + 64], ds, preferred_element_type=F32).astype(BF))
        if s == 0:
            dv0, dk0 = dvh, dkh
        sums = []
        for d in range(-3, 4):
            total = None
            for bj in range(4):
                bi = bj - d
                if 0 <= bi < 4:
                    block = ds32[128 * bj : 128 * bj + 128, 128 * bi : 128 * bi + 128]
                    total = block if total is None else total + block
            sums.append(total)
        for d in range(7):
            acc[s, d] = jnp.where(r == 0, jnp.zeros((128, 128), F32), acc[s, d]) + sums[d]
    dq = jnp.concatenate(dqs, axis=0).T
    dk = jnp.where(lane < 64, dk0, dkh).astype(BF)
    dv = jnp.where(lane < 64, dv0, dvh).astype(BF)
    d_all = jnp.concatenate([dq, dk, dv], axis=1)
    d_ref[...] = d_all
    part = jnp.dot(nt_ref[...], d_all, preferred_element_type=F32)

    @pl.when(r == 0)
    def _():
        gacc[...] = part

    @pl.when(r == 1)
    def _():
        g = (gacc[...] + part).astype(BF)
        share(place_ref[0] & 1, g, keep_ref, send_ref)
        up = upper()
        for s in range(2):
            rows = []
            for e in range(8):
                a = acc[s, e] if e < 7 else jnp.zeros((128, 128), F32)
                b = acc[s, e - 1] if e > 0 else jnp.zeros((128, 128), F32)
                c = jnp.where(up, a, b)
                total = c[0:8]
                for g8 in range(1, 16):
                    total = total + pltpu.roll(c[8 * g8 : 8 * g8 + 8], 128 - 8 * g8, 1)
                rows.append(total)
            diag_ref[0, s] = jnp.concatenate(rows, axis=1)


def share(b, g, keep_ref, send_ref):
    for a in range(2):
        even = g[(2 * a) * 192 : (2 * a + 1) * 192]
        odd = g[(2 * a + 1) * 192 : (2 * a + 2) * 192]
        keep_ref[a] = jnp.where(b == 0, even, odd)
        send_ref[a] = jnp.where(b == 0, odd, even)


def attn_bwd(place, qkv, do, ot, e, li, nt, first, count, earlier=()):
    return pl.pallas_call(
        attn_bwd_kernel,
        grid=(count, 2),
        in_specs=[
            SMEM,
            pl.BlockSpec((SEQ, 384), lambda p, r: (r, first + p)),
            pl.BlockSpec((SEQ, 128), lambda p, r: (r, first + p)),
            pl.BlockSpec((128, SEQ), lambda p, r: (p, r)),
            pl.BlockSpec((1, 2, SEQ, SEQ), lambda p, r: (r, p, 0, 0)),
            pl.BlockSpec((1, 2, 8, SEQ), lambda p, r: (r, p, 0, 0)),
            pl.BlockSpec((D, SEQ), lambda p, r: (0, r)),
        ]
        + [HBM] * len(earlier),
        out_specs=[
            pl.BlockSpec((SEQ, 384), lambda p, r: (r, p)),
            pl.BlockSpec((2, 192, 384), lambda p, r: (0, 0, p)),
            pl.BlockSpec((2, 192, 384), lambda p, r: (0, 0, p)),
            pl.BlockSpec((1, 2, 8, 1024), lambda p, r: (p, 0, 0, 0)),
        ],
        out_shape=[
            sds((T, 384 * count), BF),
            sds((2, 192, 384 * count), BF),
            sds((2, 192, 384 * count), BF),
            sds((count, 2, 8, 1024), F32),
        ],
        scratch_shapes=[pltpu.VMEM((2, 7, 128, 128), F32), pltpu.VMEM((D, 384), F32)],
        compiler_params=params(40),
        cost_estimate=cost(4e9 * count, 3e6 * count),
        name="attn_bwd",
    )(place, qkv, do, ot, e, li, nt, *earlier)


FC = 512
FSTEPS = FF // FC


def ffn_kernel(place_ref, x_ref, gain_ref, mt_ref, *rest):
    o_refs, rest = rest[:PARTS], rest[PARTS:]
    pieces, (x2_ref, nt_ref, gp_ref, acts_ref, xs_ref, wo, wi, n2, sems) = rest[:6], rest[6:]
    f, t = place_ref[0], place_ref[1]
    step = pl.program_id(0)

    @pl.when(step == 0)
    def _():
        fetch(pieces, f, t, 96, 0, 96, pl.ds(0, D), wo, pl.ds(0, D), sems.at[FSTEPS])
        for c in range(FSTEPS):
            fetch(pieces, f, t, 96, 0, 96, pl.ds(D + c * FC, FC), wi.at[c], pl.ds(0, FC), sems.at[c])
        landed(wo, sems.at[FSTEPS])
        o = jnp.concatenate([ref[...] for ref in o_refs], axis=1)
        x2 = x_ref[...].astype(F32) + jnp.dot(o, wo[...], preferred_element_type=F32)
        x2_ref[...] = x2
        n = norm(x2, gain_ref[...])[2]
        n2[...] = n
        nt_ref[...] = n.T
        hi = x2.astype(BF)
        lo = (x2 - hi.astype(F32)).astype(BF)
        mt = mt_ref[...]
        xs_ref[...] = jnp.dot(mt, hi, preferred_element_type=F32) + jnp.dot(mt, lo, preferred_element_type=F32)

    landed(wi.at[step], sems.at[step])
    u = jnp.dot(n2[...], wi[step], preferred_element_type=F32)
    u2 = u * u
    half = 0.5 + 0.5 * jnp.tanh(u * (GELU_C + (GELU_C * 0.044715) * u2))
    act = u * half
    gp_ref[...] = (half + act * (1.0 - half) * (2 * GELU_C + (6 * GELU_C * 0.044715) * u2)).astype(BF)
    acts_ref[...] = jnp.dot(mt_ref[...], act.astype(BF), preferred_element_type=F32)


def ffn_call(place, x, gain, member_t, o_parts, pieces):
    return pl.pallas_call(
        ffn_kernel,
        grid=(FSTEPS,),
        in_specs=[SMEM, whole((T, D)), whole((1, D)), whole((SLOTS, T))]
        + [whole(o.shape) for o in o_parts]
        + [HBM] * 6,
        out_specs=[
            whole((T, D)),
            whole((D, T)),
            pl.BlockSpec((T, FC), lambda c: (0, c)),
            pl.BlockSpec((SLOTS, FC), lambda c: (0, c)),
            whole((SLOTS, D)),
        ],
        out_shape=[sds((T, D), F32), sds((D, T), BF), sds((T, FF), BF), sds((SLOTS, FF), F32), sds((SLOTS, D), F32)],
        scratch_shapes=[
            pltpu.VMEM((D, D), BF),
            pltpu.VMEM((FSTEPS, D, FC), BF),
            pltpu.VMEM((T, D), BF),
            pltpu.SemaphoreType.DMA((FSTEPS + 1,)),
        ],
        compiler_params=params(56),
        cost_estimate=cost(1.2e10, 2e7),
        name="ffn_fwd",
    )(place, x, gain, member_t, *o_parts, *pieces)


def pooled_kernel(place_ref, acts_ref, xs_ref, info_ref, *rest):
    pieces, (buf_ref, hi_ref, wf, sem) = rest[:6], rest[6:]
    f, t = place_ref[0], place_ref[1]
    fetch(pieces, f, t, 480, 0, 384, pl.ds(0, D), wf, pl.ds(0, D), sem)
    acts = acts_ref[...]
    hi = acts.astype(BF)
    lo = (acts - hi.astype(F32)).astype(BF)
    hi_ref[...] = hi
    info = info_ref[...]
    landed(wf, sem)
    both = jnp.dot(jnp.concatenate([hi, lo], axis=0), wf[...], preferred_element_type=F32)
    pooled = (xs_ref[...] + both[:SLOTS] + both[SLOTS:]) / jnp.maximum(info[:, 0:1], 1.0)
    out = jnp.concatenate([pooled, info], axis=1)
    packed = [out[8 * m : 8 * m + 1, 128 * c : 128 * c + 128] for m in range(MB) for c in range(PAY // 128)]
    packed = jnp.concatenate(packed + [jnp.zeros((SLOTS - len(packed), 128), F32)], axis=0)
    buf_ref[...] = jnp.concatenate([out, packed], axis=1).astype(BF)


def pooled_call(place, acts, xs, info, pieces):
    return pl.pallas_call(
        pooled_kernel,
        in_specs=[SMEM, VMEM, VMEM, VMEM] + [HBM] * 6,
        out_specs=[VMEM, VMEM],
        out_shape=[sds((SLOTS, FULL), BF), sds((SLOTS, FF), BF)],
        scratch_shapes=[pltpu.VMEM((FF, D), BF), pltpu.SemaphoreType.DMA],
        compiler_params=params(40),
        cost_estimate=cost(2e9, 5e6),
        name="pooled",
    )(place, acts, xs, info, *pieces)


def loss_kernel(rows, place_ref, own_buf, mate_buf, *rest):
    pieces, (loss_ref, own_ref, all_ref, gproj_ref, scr, wp, gp_scr, gz_scr, loss_scr, sems) = rest[:6], rest[6:]
    f, t, z = place_ref[0], place_ref[1], place_ref[2]
    fetch(pieces, f, t, 480, 384, 96, pl.ds(0, D), wp, pl.ds(0, D), sems.at[0])
    nq, np_ = rows * SLOTS, rows * MB
    for m, buf in enumerate((own_buf, mate_buf)):
        for k in range(rows // 2):
            row = (z ^ (k >> 1)) * 4 + (f ^ (2 * (k & 1)) ^ m)
            pltpu.make_async_copy(
                buf.at[pl.ds(k * SLOTS, SLOTS)], scr.at[pl.ds(pl.multiple_of(row * SLOTS, SLOTS), SLOTS)], sems.at[1]
            ).start()
    landed(scr, sems.at[1])
    blocks = scr[:, PAY:]
    chunks = []
    p_row = lax.broadcasted_iota(jnp.int32, (np_, nq), 0)
    q_at = lax.broadcasted_iota(jnp.int32, (np_, nq), 1)
    for c in range(PAY // 128):
        picker = (q_at == (p_row // MB) * SLOTS + (p_row % MB) * (PAY // 128) + c).astype(BF)
        chunks.append(jnp.dot(picker, blocks, preferred_element_type=F32).astype(BF))
    p_all = jnp.concatenate(chunks, axis=1)
    q_all = scr[:, :PAY]
    both = jnp.concatenate([q_all[:, :D], p_all[:, :D]], axis=0)
    extra = jnp.concatenate([q_all[:, D:], p_all[:, D:]], axis=0).astype(F32)
    landed(wp, sems.at[0])
    proj = wp[...]
    zz = jnp.dot(both, proj, preferred_element_type=F32)
    inv = lax.rsqrt(jnp.sum(zz * zz, axis=-1, keepdims=True) + EPSILON)
    w = zz * inv
    e = w.astype(BF)
    eq, ep = e[:nq], e[nq:]
    logits = LOGIT_SCALE * lax.dot_general(eq, ep, NT, preferred_element_type=F32)
    q_row = lax.broadcasted_iota(jnp.int32, (nq, np_), 0)
    p_col = lax.broadcasted_iota(jnp.int32, (nq, np_), 1)
    same = (q_row // QSEG) % MB == p_col % MB
    logits = jnp.where(same, logits, -1e30)
    top = jnp.max(logits, axis=-1, keepdims=True)
    log_total = top + jnp.log(jnp.sum(jnp.exp(logits - top), axis=-1, keepdims=True))
    positive = extra[:nq, 1:2].astype(jnp.int32)
    hot = jnp.where(same & (p_col // MB == positive), 1.0, 0.0)
    loss = log_total - jnp.sum(logits * hot, axis=-1, keepdims=True)
    gl = LOSS_SCALE * (jnp.exp(logits - log_total) - hot)
    g_eq = LOGIT_SCALE * jnp.dot(gl, ep.astype(F32), precision=HIGHEST, preferred_element_type=F32)
    g_ep = LOGIT_SCALE * lax.dot_general(gl, eq.astype(F32), TN, precision=HIGHEST, preferred_element_type=F32)
    ge = jnp.concatenate([g_eq, g_ep], axis=0)
    gz = (inv * (ge - w * jnp.sum(w * ge, axis=-1, keepdims=True))).astype(BF)
    count = jnp.maximum(extra[:, 0:1], 1.0)
    g_x3 = lax.dot_general(gz, proj, NT, preferred_element_type=F32) / count
    all_ref[...] = g_x3.astype(BF)
    row = z * 4 + f
    gz_scr[...] = gz[:nq]
    loss_scr[...] = jnp.broadcast_to(
        jnp.where(lax.broadcasted_iota(jnp.int32, (nq, 128), 1) == 0, loss, count[:nq]), (nq, 128)
    )
    mine = pl.ds(pl.multiple_of(row * SLOTS, SLOTS), SLOTS)
    slot = lax.broadcasted_iota(jnp.int32, (SLOTS, np_), 0)
    chosen = (slot % QSEG == 0) & (lax.broadcasted_iota(jnp.int32, (SLOTS, np_), 1) == row * MB + slot // QSEG)
    own_p = jnp.dot(chosen.astype(F32), g_x3[nq:], precision=HIGHEST, preferred_element_type=F32)
    own_q = lax.dot_general(gz_scr[mine, :], proj, NT, preferred_element_type=F32) / loss_scr[mine, 1:2]
    own_ref[...] = jnp.where(t == 0, own_q, own_p)
    loss_ref[...] = loss_scr[mine, :]
    gp_scr[...] = lax.dot_general(both, gz, TN, preferred_element_type=F32)
    gproj_ref[...] = gp_scr[pl.ds(pl.multiple_of(f * 192, 192), 192), :]


def loss_call(place, own_buf, mate_buf, pieces, rows):
    nq = rows * SLOTS
    return pl.pallas_call(
        functools.partial(loss_kernel, rows),
        in_specs=[SMEM] + [HBM] * 8,
        out_specs=[VMEM] * 4,
        out_shape=[sds((SLOTS, 128), F32), sds((SLOTS, D), F32), sds((nq + rows * MB, D), BF), sds((192, D), F32)],
        scratch_shapes=[
            pltpu.VMEM((nq, FULL), BF),
            pltpu.VMEM((D, D), BF),
            pltpu.VMEM((D, D), F32),
            pltpu.VMEM((nq, D), BF),
            pltpu.VMEM((nq, 128), F32),
            pltpu.SemaphoreType.DMA((2,)),
        ],
        compiler_params=params(60),
        cost_estimate=cost(5e9, 1e6),
        name="loss",
    )(place, own_buf, mate_buf, *pieces)


def ffn_bwd_kernel(place_ref, own_ref, m2_ref, gp_ref, nt_ref, *rest):
    mids, outs, (keep_ref, send_ref, gn_ref, wi, wf, gf, sems) = rest[:6], rest[6:12], rest[12:]
    f, t = place_ref[0], place_ref[1]
    step = pl.program_id(0)

    @pl.when(step == 0)
    def _():
        fetch(outs, f, t, 480, 0, 384, pl.ds(0, D), wf, pl.ds(0, D), sems.at[FSTEPS])
        for c in range(FSTEPS):
            fetch(mids, f, t, 96, 0, 96, pl.ds(D + c * FC, FC), wi.at[c], pl.ds(0, FC), sems.at[c])
        gf[...] = own_ref[...].astype(BF)
        gn_ref[...] = jnp.zeros_like(gn_ref)
        landed(wf, sems.at[FSTEPS])

    rows = wf[pl.ds(pl.multiple_of(step * FC, FC), FC), :]
    gh = lax.dot_general(gf[...], rows, NT, preferred_element_type=F32)
    hi = gh.astype(BF)
    lo = (gh - hi.astype(F32)).astype(BF)
    wide = jnp.dot(m2_ref[...], jnp.concatenate([hi, lo], axis=0), preferred_element_type=F32)
    gu = (wide * gp_ref[...].astype(F32)).astype(BF)
    g = jnp.dot(nt_ref[...], gu, preferred_element_type=F32).astype(BF)
    share(f & 1, g, keep_ref, send_ref)
    landed(wi.at[step], sems.at[step])
    gn_ref[...] += lax.dot_general(gu, wi[step], NT, preferred_element_type=F32)


def ffn_bwd_call(place, own, member2, gp, n2t, mids, outs):
    return pl.pallas_call(
        ffn_bwd_kernel,
        grid=(FSTEPS,),
        in_specs=[SMEM, whole((SLOTS, D)), whole((T, 2 * SLOTS)), pl.BlockSpec((T, FC), lambda c: (0, c)), whole((D, T))]
        + [HBM] * 12,
        out_specs=[
            pl.BlockSpec((2, 192, FC), lambda c: (0, 0, c)),
            pl.BlockSpec((2, 192, FC), lambda c: (0, 0, c)),
            whole((T, D)),
        ],
        out_shape=[sds((2, 192, FF), BF), sds((2, 192, FF), BF), sds((T, D), F32)],
        scratch_shapes=[
            pltpu.VMEM((FSTEPS, D, FC), BF),
            pltpu.VMEM((FF, D), BF),
            pltpu.VMEM((SLOTS, D), BF),
            pltpu.SemaphoreType.DMA((FSTEPS + 1,)),
        ],
        compiler_params=params(56),
        cost_estimate=cost(1.2e10, 2e7),
        name="ffn_bwd",
    )(place, own, member2, gp, n2t, *mids, *outs)


def mid_kernel(place_ref, gn_ref, x2_ref, gain_ref, own_ref, m2_ref, *rest):
    ots, rest = rest[:PARTS], rest[PARTS:]
    pieces, (gx_ref, go_ref, keep_ref, send_ref, wo, sem) = rest[:6], rest[6:]
    f, t = place_ref[0], place_ref[1]
    fetch(pieces, f, t, 96, 0, 96, pl.ds(0, D), wo, pl.ds(0, D), sem)
    own = own_ref[...]
    hi = own.astype(BF)
    lo = (own - hi.astype(F32)).astype(BF)
    g_x3 = jnp.dot(m2_ref[...], jnp.concatenate([hi, lo], axis=0), preferred_element_type=F32)
    gain = gain_ref[...]
    inv, scaled, _ = norm(x2_ref[...], gain)
    g_x2 = g_x3 + norm_back(gn_ref[...], inv, scaled, gain)
    gx_ref[...] = g_x2
    ga = g_x2.astype(BF)
    landed(wo, sem)
    go_ref[...] = lax.dot_general(ga, wo[...], NT, preferred_element_type=F32).astype(BF)
    ot = jnp.concatenate([ref[...] for ref in ots], axis=0)
    g = jnp.dot(ot, ga, preferred_element_type=F32).astype(BF)
    share(f & 1, g, keep_ref, send_ref)


def mid_call(place, gn, x2, gain, own, member2, ots, pieces):
    return pl.pallas_call(
        mid_kernel,
        in_specs=[SMEM] + [VMEM] * (5 + PARTS) + [HBM] * 6,
        out_specs=[VMEM] * 4,
        out_shape=[sds((T, D), F32), sds((T, D), BF), sds((2, 192, D), BF), sds((2, 192, D), BF)],
        scratch_shapes=[pltpu.VMEM((D, D), BF), pltpu.SemaphoreType.DMA],
        compiler_params=params(56),
        cost_estimate=cost(3e9, 1e7),
        name="attn_out_bwd",
    )(place, gn, x2, gain, own, member2, *ots, *pieces)


def token_kernel(place_ref, gx_ref, x_ref, gain_ref, *rest):
    d_refs, rest = rest[:PARTS], rest[PARTS:]
    pieces, (out_ref, w, sem) = rest[:6], rest[6:]
    f, t = place_ref[0], place_ref[1]
    r = pl.program_id(0)

    @pl.when(r == 0)
    def _():
        fetch(pieces, f, t, 96, 0, 96, pl.ds(0, 3 * D), w, pl.ds(0, 3 * D), sem)
        landed(w, sem)

    d_all = jnp.concatenate([ref[...] for ref in d_refs], axis=1)
    g_n1 = lax.dot_general(d_all, w[...], NT, preferred_element_type=F32)
    gain = gain_ref[...]
    inv, scaled, _ = norm(x_ref[...].astype(F32), gain)
    out_ref[...] = (gx_ref[...] + norm_back(g_n1, inv, scaled, gain)).astype(BF)


def token_call(place, gx, x, gain, d_parts, pieces):
    row = lambda r: (r, 0)
    return pl.pallas_call(
        token_kernel,
        grid=(2,),
        in_specs=[SMEM, pl.BlockSpec((SEQ, D), row), pl.BlockSpec((SEQ, D), row), whole((1, D))]
        + [pl.BlockSpec((SEQ, d.shape[1]), row) for d in d_parts]
        + [HBM] * 6,
        out_specs=pl.BlockSpec((SEQ, D), row),
        out_shape=sds((T, D), BF),
        scratch_shapes=[pltpu.VMEM((D, 3 * D), BF), pltpu.SemaphoreType.DMA],
        compiler_params=params(56),
        cost_estimate=cost(4e9, 1e7),
        name="token_grad",
    )(place, gx, x, gain, *d_parts, *pieces)


def swap(block, axis, bit):
    size = lax.axis_size(axis)
    return lax.ppermute(block, axis, [(i, i ^ bit) for i in range(size)])


def after(block, *earlier):
    def kernel(*refs):
        pass

    return pl.pallas_call(
        kernel,
        in_specs=[HBM] * (1 + len(earlier)),
        out_specs=HBM,
        out_shape=sds(block.shape, block.dtype),
        input_output_aliases={0: 0},
        name="after",
    )(block, *earlier)


def pack_kernel(plan, place_ref, *refs):
    ins, own_ref, sent_ref = refs[:-2], refs[-2], refs[-1]
    t = place_ref[1]
    for src, rows, src_cols, dst_rows, dst_cols in plan:
        block = ins[src][pl.ds(rows[0], rows[1]), pl.ds(*src_cols)].astype(BF)
        own_ref[pl.ds(*dst_rows), pl.ds(*dst_cols)] = block
    half = own_ref.shape[0] // 2
    sent_ref[...] = own_ref[pl.ds(pl.multiple_of(t * half, 32), half), :]


def pack_call(place, plan, arrays, shape):
    return pl.pallas_call(
        functools.partial(pack_kernel, plan),
        in_specs=[SMEM] + [VMEM] * len(arrays),
        out_specs=[VMEM, VMEM],
        out_shape=[sds(shape, BF), sds((shape[0] // 2, shape[1]), BF)],
        compiler_params=params(40),
        cost_estimate=cost(1e6, 6 * shape[0] * shape[1]),
        name="pack",
    )(place, *arrays)


def gather_start(own, sent):
    return own, swap(own, "fsdp", 1), swap(sent, "fsdp", 2)


def gather_rest(own, mate, near):
    far = swap(near, "tower", 1)
    return own, mate, near, far, swap(near, "fsdp", 1), swap(far, "fsdp", 1)


def pick(parts, index):
    return lax.dynamic_index_in_dim(parts, index, 0, keepdims=False)


def rounded(v):
    return lax.reduce_precision(v, 8, 7)


def plus(a, b):
    return a.astype(F32) + b.astype(F32)


def mesh_step(keep, got):
    a = lax.axis_index("fsdp") // 2
    out = plus(pick(keep, 1 - a), pick(got, 1 - a)).astype(BF)
    return plus(pick(keep, a), pick(got, a)), out


def tower_step(mine, got):
    t = lax.axis_index("tower")
    cols = mine.shape[-1]
    mine, got = mine.reshape(2, 96, cols), got.reshape(2, 96, cols)
    out = plus(pick(mine, 1 - t), pick(got, 1 - t)).astype(BF)
    return plus(pick(mine, t), pick(got, t)), out


def dp_sum(total):
    bit = 1
    while bit < lax.axis_size("dp"):
        total = plus(total, swap(total, "dp", bit)).astype(BF)
        bit *= 2
    return total


def dp_sum_halves(mine, got):
    z = lax.axis_index("dp")
    bits = [1 << i for i in range(lax.axis_size("dp").bit_length() - 1)]
    for bit in bits:
        cols = mine.shape[-1] // 2
        up = (z // bit) % 2
        part = lambda v, i: lax.dynamic_slice_in_dim(v, i * cols, cols, 1)
        out = plus(part(mine, 1 - up), part(got, 1 - up)).astype(BF)
        mine = plus(part(mine, up), part(got, up))
        got = swap(out, "dp", bit)
    total = lax.optimization_barrier(plus(mine, got).astype(BF))
    for bit in reversed(bits):
        up = (z // bit) % 2
        other = swap(total, "dp", bit)
        total = jnp.concatenate([jnp.where(up == 0, total, other), jnp.where(up == 0, other, total)], axis=1)
    return total


def tower_join(total):
    t = lax.axis_index("tower")
    total = lax.optimization_barrier(total)
    other = swap(total, "tower", 1)
    return jnp.concatenate([jnp.where(t == 0, total, other), jnp.where(t == 0, other, total)], axis=0)


def sum_all(v):
    for axis, bit in (("fsdp", 1), ("fsdp", 2), ("tower", 1)):
        v = v + swap(v, axis, bit)
    bit = 1
    while bit < lax.axis_size("dp"):
        v = v + swap(v, "dp", bit)
        bit *= 2
    return v


def gather_rows(buf, is_query):
    got = swap(buf, "tower", 1)
    buf = jnp.concatenate(
        [jnp.where(is_query, buf[:, :PAY], got[:, :PAY]), jnp.where(is_query, got[:, PAY:], buf[:, PAY:])], axis=1
    )
    n_dp = lax.axis_size("dp")
    if n_dp == 4:
        parts = [buf]
        for k in range(1, 8):
            move = [(i, i ^ ((k >> 1) * 4 + (k & 1) * 2)) for i in range(16)]
            parts.append(lax.ppermute(buf, ("dp", "fsdp"), move))
        buf = jnp.concatenate(parts, axis=0)
    else:
        buf = jnp.concatenate([buf, swap(buf, "fsdp", 2)], axis=0)
        bit = 1
        while bit < n_dp:
            buf = jnp.concatenate([buf, swap(buf, "dp", bit)], axis=0)
            bit *= 2
    return buf, swap(buf, "fsdp", 1)


def interleave(parts):
    rows = parts[0].shape[0]
    return jnp.stack([v.reshape(rows, PAIRS, 128) for v in parts], axis=2).reshape(rows, 3 * D)


def local(
    tokens_in,
    query_lengths,
    positive_ids,
    gain_attn,
    gain_ffn,
    w_query,
    w_key,
    w_value,
    w_out,
    rel_bias,
    w_in,
    w_ffn_out,
    w_proj,
):
    f = lax.axis_index("fsdp")
    t = lax.axis_index("tower")
    z = lax.axis_index("dp")
    rows = lax.axis_size("dp") * 4
    is_query = t == 0
    place = jnp.stack([f, t, z]).astype(jnp.int32)

    small = jnp.concatenate([gain_attn, gain_ffn, rel_bias.reshape(-1), jnp.zeros((32,), F32)])
    small = small.astype(BF).reshape(1, 512)
    small = jnp.concatenate([small, swap(small, "fsdp", 1)], axis=0)
    small = jnp.concatenate([small, swap(small, "fsdp", 2)], axis=0)
    small = jnp.stack([pick(small, i ^ f) for i in range(4)])
    gain_one = small[:, :192].reshape(1, D).astype(F32)
    gain_two = small[:, 192:384].reshape(1, D).astype(F32)
    table = small[:, 384:480].reshape(NB, H)

    plan = [
        (i, (0, 192), (128 * p, 128), (0, 192), (384 * p + 128 * i, 128)) for p in range(PAIRS) for i in range(3)
    ]
    own1, sent1 = pack_call(place, plan, (w_query, w_key, w_value), (192, 3 * D))
    plan = [(0, (0, 192), (0, D), (0, 192), (0, D)), (1, (0, 192), (0, FF), (0, 192), (D, FF))]
    own2, sent2 = pack_call(place, plan, (w_out, w_in), (192, D + FF))
    plan = []
    for h in range(2):
        plan.append((0, (384 * h, 384), (0, D), (480 * h, 384), (0, D)))
        plan.append((1, (96 * h, 96), (0, D), (480 * h + 384, 96), (0, D)))
    own3, sent3 = pack_call(place, plan, (w_ffn_out, w_proj), (960, D))
    first = gather_start(own1, sent1)
    middle = gather_start(own2, after(sent2, first[2]))
    last = gather_start(own3, after(sent3, middle[2]))
    first, middle, last = gather_rest(*first), gather_rest(*middle), gather_rest(*last)

    lengths = query_lengths[:, 0]
    ends = jnp.cumsum(lengths, axis=-1)
    places = lax.broadcasted_iota(jnp.int32, (MB, SEQ, QSEG), 1)
    segment = jnp.where(is_query, jnp.sum((places >= ends[:, None, :]).astype(jnp.int32), axis=-1), 0)
    slot_ids = lax.broadcasted_iota(jnp.int32, (MB, QSEG), 1)
    counts = jnp.where(is_query, lengths, jnp.where(slot_ids < 1, SEQ, 0))
    seg = segment.reshape(T)
    lane = lax.broadcasted_iota(jnp.int32, (T, 128), 1) % 64
    hot_seg = lane == seg[:, None]
    fq = jnp.where(hot_seg, 1.0, 0.0).astype(BF)
    fk = jnp.where((lane < QSEG) & ~hot_seg, -1e30, 0.0).astype(BF)
    slot_of = seg + QSEG * (lax.broadcasted_iota(jnp.int32, (T,), 0) // SEQ)
    member2 = (slot_of[:, None] == lax.broadcasted_iota(jnp.int32, (T, 2 * SLOTS), 1) % SLOTS).astype(BF)
    member_t = (slot_of[None, :] == lax.broadcasted_iota(jnp.int32, (SLOTS, T), 0)).astype(BF)
    info = jnp.concatenate(
        [
            counts.reshape(SLOTS, 1).astype(F32),
            positive_ids.reshape(SLOTS, 1).astype(F32),
            jnp.zeros((SLOTS, 126), F32),
        ],
        axis=1,
    )
    bias = bias_blocks(jnp.pad(table.T, ((0, 4), (0, 0))), diag_hot())

    x = tokens_in.reshape(T, D)
    n1, n1t = norm_call(x, gain_one)
    qkv = qkv_call(place, n1, first)
    heads = [attn_fwd(qkv, fq, fk, bias, i * PER, PER) for i in range(PARTS)]
    x2, n2t, gp, acts, xs = ffn_call(place, x, gain_two, member_t, [h[0] for h in heads], middle)
    buf, acts_hi = pooled_call(place, acts, xs, info, last)
    own_buf, mate_buf = gather_rows(buf, is_query)
    loss, own, gf_all, grad_proj = loss_call(place, own_buf, mate_buf, last, rows)
    query_loss = loss[:, 0].reshape(MB, 1, QSEG)
    acts_all = lax.all_gather(acts_hi, ALL, axis=0, tiled=True)

    keep_i, send_i, g_n2 = ffn_bwd_call(place, own, member2, gp, n2t, middle, last)
    got_i = swap(send_i, "fsdp", 1)
    g_x2, go, keep_o, send_o = mid_call(place, g_n2, x2, gain_two, own, member2, [h[1] for h in heads], middle)
    mine_i, out_i = mesh_step(keep_i, got_i)
    got_i = swap(out_i, "fsdp", 2)
    back = lambda i, *earlier: attn_bwd(place, qkv, go, *heads[i][1:], n1t, i * PER, PER, earlier)
    cat = lambda *v: jnp.concatenate(v, axis=2)
    d_a, keep_a, send_a, diag_a = back(0, out_i)
    d_b, keep_b, send_b, diag_b = back(1, keep_a)
    keep_a, send_a = cat(keep_o, keep_a, keep_b), cat(send_o, send_a, send_b)
    got_a = swap(send_a, "fsdp", 1)
    d_c, keep_c, send_c, diag_c = back(2, send_a)
    got_c = swap(send_c, "fsdp", 1)
    mine_i, out_i = tower_step(mine_i, got_i)
    got_i = swap(out_i, "tower", 1)
    mine_a, out_a = mesh_step(keep_a, got_a)
    got_a = swap(out_a, "fsdp", 2)
    mine_c, out_c = mesh_step(keep_c, got_c)
    got_c = swap(after(out_c, out_a), "fsdp", 2)
    grad_in = tower_join(dp_sum_halves(mine_i, got_i))
    mine_a, out_a = tower_step(mine_a, got_a)
    got_a = swap(out_a, "tower", 1)
    grad_a = tower_join(dp_sum(plus(mine_a, got_a).astype(BF)))
    mine_c, out_c = tower_step(mine_c, got_c)
    got_c = swap(out_c, "tower", 1)
    grad_c = tower_join(dp_sum(plus(mine_c, got_c).astype(BF)))
    diag = jnp.concatenate([diag_a, diag_b, diag_c], axis=0).reshape(H, 8192)
    grad_table = sum_all(jnp.einsum("hc,cb->bh", diag, diag_hot2(), precision=HIGHEST))
    grad_tokens = token_call(place, g_x2, x, gain_one, (d_a, d_b, d_c), first).reshape(1, MB, 1, SEQ, D)

    acts_mine = lax.dynamic_slice_in_dim(acts_all, f * D, D, 1).reshape(2, rows * MB, QSEG, D)
    acts_mine = jnp.concatenate([acts_mine[0].reshape(rows * SLOTS, D), acts_mine[1, :, 0]], axis=0)
    grad_ffn_out = lax.dot_general(acts_mine, gf_all, TN, preferred_element_type=F32)
    grad_out = grad_a[:, :D].astype(F32)
    grad_qkv = jnp.concatenate([grad_a[:, D:], grad_c], axis=1).astype(F32)
    grad_in = grad_in.astype(F32)
    low = lambda g: g.astype(BF).astype(F32)
    grad_gain_one = jnp.sum(grad_qkv * own1.astype(F32), axis=1) / low(gain_attn)
    grad_gain_two = jnp.sum(grad_in * own2[:, D:].astype(F32), axis=1) / low(gain_ffn)
    by_kind = grad_qkv.reshape(192, PAIRS, 3, 128)
    return (
        query_loss,
        grad_tokens,
        grad_gain_one,
        grad_gain_two,
        by_kind[:, :, 0].reshape(192, D),
        by_kind[:, :, 1].reshape(192, D),
        by_kind[:, :, 2].reshape(192, D),
        grad_out,
        lax.dynamic_slice_in_dim(grad_table, f * 8, 8, 0),
        grad_in,
        grad_ffn_out,
        grad_proj,
    )


def solution(mesh):
    rows = P(None, ("dp", "fsdp"), None)
    tokens = P("tower", None, ("dp", "fsdp"), None, None)
    vec, mat = P("fsdp"), P("fsdp", None)
    return jax.shard_map(
        local,
        mesh=mesh,
        in_specs=(tokens, rows, rows, vec, vec) + (mat,) * 8,
        out_specs=(rows, tokens, vec, vec) + (mat,) * 8,
        check_vma=False,
    )
```

time: 475 us -> 374 us (0.79)
  Pallas kernels: 54.4 us -> 137 us
  matrix products: 83 us -> 3.49 us
  blocking collectives: 62.4 us -> 0 us
  waiting for transfers between devices: 138 us -> 75.7 us
  starting transfers between devices: 28 us -> 55.6 us
  other arithmetic: 36.4 us -> 24.6 us
  local copies, waits for them, and re-layouts: 50 us -> 58.4 us
    pallas_call x4 -> x21, Pallas kernels: 54.4 us -> 137 us  [the longest x3 31.3 us: attn_bwd(): pl.pallas_call(attn_bwd_kernel, grid=(count, 2), in_specs=[SMEM, pl.Block...]
    dot_general x21 -> x2, matrix products: 83 us -> 3.49 us  [the longest x1 2.2 us: local(): lax.dot_general(acts_mine, gf_all, TN, preferred_element_type=F32)]
    ppermute x37 -> x44, waiting for transfers between devices: 138 us -> 70.2 us  [swap(): return lax.ppermute(block, axis, [(i, i ^ bit) for i in range(size)])]
    psum x1 -> x0, blocking collectives: 46.2 us -> none  [local(): tiny = lax.psum(tiny, ALL)]
    unnamed x92 -> x173, local copies, waits for them, and re-layouts: 12.3 us -> 45.9 us
    dynamic_update_slice x20 -> x0, local copies, waits for them, and re-layouts: 20.4 us -> none  [gather_group(): full = lax.dynamic_update_slice_in_dim(full, piece, start, 0)]
    ppermute x37 -> x44, starting transfers between devices: 28 us -> 44.4 us  [swap(): return lax.ppermute(block, axis, [(i, i ^ bit) for i in range(size)])]
    all_gather x1 -> x0, blocking collectives: 16.2 us -> none  [local(): small = lax.all_gather(small, 'fsdp', axis=0)]
  transfers between devices with their start and end apart: 38 -> 52, of which waited for: 13 -> 19; matrix products, arithmetic and copies ran while one was open for 32% -> 9% of each run, Pallas kernels for 12% -> 28%
where the time goes in v2:
time: 374 us; the launch traced here: 370 us
  Pallas kernels  137 us (37%)
  waiting for transfers between devices  75.7 us (20%)
  local copies, waits for them, and re-layouts  58.4 us (16%)
  starting transfers between devices  55.6 us (15%)
  other arithmetic  24.6 us (7%)
  between operations  15.3 us (4%)
    ppermute x44, waiting for transfers between devices, swap(): return lax.ppermute(block, axis, [(i, i ^ bit) for i in range(size)])  70.2 us
    unnamed x173, local copies, waits for them, and re-layouts  45.9 us
    ppermute x44, starting transfers between devices, swap(): return lax.ppermute(block, axis, [(i, i ^ bit) for i in range(size)])  44.4 us
    pallas_call x3, Pallas kernels, attn_bwd(): pl.pallas_call(attn_bwd_kernel, grid=(count, 2), in_specs=[SMEM, pl.Block...  31.3 us
    pallas_call x1, Pallas kernels, ffn_bwd_call(): pl.pallas_call(ffn_bwd_kernel, grid=(FSTEPS,), in_specs=[SMEM, whole((SLO...  21.6 us
    pallas_call x3, Pallas kernels, attn_fwd(): pl.pallas_call(attn_fwd_kernel, grid=(count, 2), in_specs=[pl.BlockSpec((...  20.7 us
    pallas_call x1, Pallas kernels, ffn_call(): pl.pallas_call(ffn_kernel, grid=(FSTEPS,), in_specs=[SMEM, whole((T, D)),...  18.2 us
    ppermute x7, starting transfers between devices, gather_rows(): parts.append(lax.ppermute(buf, ('dp', 'fsdp'), move))  11.2 us
  transfers between devices with their start and end apart: 52, of which 19 were waited for; matrix products, arithmetic and copies ran while one was open for 9% of the time, Pallas kernels for 28%

profile of v2, /device:TPU:0, one launch (start us, length us, event | category | flops | bytes accessed | tf_op | source)
XLA Modules:
  0.0 369.8 jit_solution(6711091459206746095)
XLA Ops:
  14.7 2.9 collective-permute-start.3
  42.7 5.0 %bias_blocks.1.bias_ref = f32[12,7,128,128]{3,2,1,0:T(8,128)} custom-call(bf16[16,32]{1,0:T(8,128)(2,1)} %pad.4.tab_ref, bf16[32,1024]{1,0:T(8,128)(2,1)} %fusion.65.hot_ref), custom_call_target="tpu_custom_call" | custom-call | flops 5000000000 | bytes 5000000 | tf_op jit(solution)/shard_map/bias_blocks/pallas_call | solution.py:96
  47.8 3.8 %collective-permute-done.8.rest_5_.refs_1_.rest_2_ = bf16[96,3840]{1,0:T(8,128)(2,1)} collective-permute-done((bf16[96,3840]{1,0:T(8,128)(2,1)}, bf16[96,3840]{1,0:T(8,128)(2,1)}, u32[]{:S(2)}, u32[]{:S(2)}) %collective-permute-start.8) | collective-permute-done | bytes 737312 | tf_op jit(solution)/shard_map/ppermute | solution.py:645
  56.9 6.3 %qkv.1.qkv_ref = bf16[1024,2304]{1,0:T(8,128)(2,1)S(1)} custom-call(s32[3]{0:T(128)S(1)} %pad_add_fusion.place_ref, bf16[1024,768]{1,0:T(8,128)(2,1)S(1)} %copy-done.43, bf16[192,2304]{1,0:T(8,128)(2,1)S(1)} %get-tuple-element.63.rest_0_.rest_3_, bf16[192,2304]{1,0:T(8,128)(2,1)} %collective-permute-done.2.rest_1_.rest_4_, bf16[96,2304]{1,0:T(8,128)(2,1)S(1)} %copy-done.20, ...), custom_call_target="tpu_custom_call" | custom-call | flops 3600000000 | bytes 10000000 | tf_op jit(solution)/shard_map/qkv/pallas_call | solution.py:171
  63.3 7.4 %attn_fwd.3 = (bf16[1024,256]{1,0:T(8,128)(2,1)S(1)}, bf16[256,1024]{1,0:T(8,128)(2,1)S(1)}, bf16[2,4,512,512]{3,2,1,0:T(8,128)(2,1)S(1)}, f32[2,4,8,512]{3,2,1,0:T(8,128)S(1)}) custom-call(bf16[1024,2304]{1,0:T(8,128)(2,1)S(1)} %qkv.1.qkv_ref, bf16[1024,128]{1,0:T(8,128)(2,1)S(1)} %copy-done.22, bf16[1024,128]{1,0:T(8,128)(2,1)S(1)} %copy-done.21, ...), custom_call_target="tpu_custom_call" | custom-call | flops 6600000000 | bytes 6000000 | tf_op jit(solution)/shard_map/attn_fwd/pallas_call | solution.py:212
  76.9 6.7 %attn_fwd.4 = (bf16[1024,256]{1,0:T(8,128)(2,1)S(1)}, bf16[256,1024]{1,0:T(8,128)(2,1)S(1)}, bf16[2,4,512,512]{3,2,1,0:T(8,128)(2,1)S(1)}, f32[2,4,8,512]{3,2,1,0:T(8,128)S(1)}) custom-call(bf16[1024,2304]{1,0:T(8,128)(2,1)S(1)} %qkv.1.qkv_ref, bf16[1024,128]{1,0:T(8,128)(2,1)S(1)} %copy-done.22, bf16[1024,128]{1,0:T(8,128)(2,1)S(1)} %copy-done.21, ...), custom_call_target="tpu_custom_call" | custom-call | flops 6600000000 | bytes 6000000 | tf_op jit(solution)/shard_map/attn_fwd/pallas_call | solution.py:212
  87.8 6.7 %attn_fwd.5 = (bf16[1024,256]{1,0:T(8,128)(2,1)S(1)}, bf16[256,1024]{1,0:T(8,128)(2,1)S(1)}, bf16[2,4,512,512]{3,2,1,0:T(8,128)(2,1)S(1)}, f32[2,4,8,512]{3,2,1,0:T(8,128)S(1)}) custom-call(bf16[1024,2304]{1,0:T(8,128)(2,1)S(1)} %qkv.1.qkv_ref, bf16[1024,128]{1,0:T(8,128)(2,1)S(1)} %copy-done.22, bf16[1024,128]{1,0:T(8,128)(2,1)S(1)} %copy-done.21, ...), custom_call_target="tpu_custom_call" | custom-call | flops 6600000000 | bytes 6000000 | tf_op jit(solution)/shard_map/attn_fwd/pallas_call | solution.py:212
  99.8 18.2 %ffn_fwd.1 = (f32[1024,768]{1,0:T(8,128)}, bf16[768,1024]{1,0:T(8,128)(2,1)}, bf16[1024,3072]{1,0:T(8,128)(2,1)}, f32[16,3072]{1,0:T(8,128)}, f32[16,768]{1,0:T(8,128)}) custom-call(s32[3]{0:T(128)} %copy-done.23, bf16[1024,768]{1,0:T(8,128)(2,1)} %bitcast.67, f32[1,768]{1,0:T(1,128)} %reshape.290.gain_ref, bf16[16,1024]{1,0:T(8,128)(2,1)} %fusion.66.mt_ref, ...), custom_call_target="tpu_custom_call" | custom-call | flops 12000000000 | bytes 20000000 | tf_op jit(solution)/shard_map/ffn_fwd/pallas_call | solution.py:382
  120.0 2.9 pooled.1
  123.6 3.4 collective-permute-done.17
  130.6 2.6 collective-permute-start.21
  133.5 3.6 collective-permute-start.23
  139.3 4.4 %collective-permute-done.24 = bf16[16,1024]{1,0:T(8,128)(2,1)S(1)} collective-permute-done((bf16[16,1024]{1,0:T(8,128)(2,1)S(1)}, bf16[16,1024]{1,0:T(8,128)(2,1)S(1)}, u32[]{:S(2)}, u32[]{:S(2)}) %collective-permute-start.24) | collective-permute-done | bytes 32800 | tf_op jit(solution)/shard_map/ppermute | solution.py:772
  145.9 7.3 %loss.1 = (f32[16,128]{1,0:T(8,128)}, f32[16,768]{1,0:T(8,128)}, bf16[288,768]{1,0:T(8,128)(2,1)}, f32[192,768]{1,0:T(8,128)}) custom-call(s32[3]{0:T(128)} %copy-done.23, bf16[128,1024]{1,0:T(8,128)(2,1)} %copy-done.71, bf16[128,1024]{1,0:T(8,128)(2,1)} %copy-done.76, bf16[960,768]{1,0:T(8,128)(2,1)} %copy-done.29, ...), custom_call_target="tpu_custom_call" | custom-call | flops 5000000000 | bytes 1000000 | tf_op jit(solution)/shard_map/loss/pallas_call | solution.py:505
  153.2 21.6 %ffn_bwd.1 = (bf16[2,192,3072]{2,1,0:T(8,128)(2,1)}, bf16[2,192,3072]{2,1,0:T(8,128)(2,1)}, f32[1024,768]{1,0:T(8,128)}) custom-call(s32[3]{0:T(128)} %copy-done.23, f32[16,768]{1,0:T(8,128)} %get-tuple-element.76.own_ref, bf16[1024,32]{1,0:T(8,128)(2,1)} %fusion.42.m2_ref, bf16[1024,3072]{1,0:T(8,128)(2,1)} %get-tuple-element.77.gp_ref, ...), custom_call_target="tpu_custom_call" | custom-call | flops 12000000000 | bytes 20000000 | tf_op jit(solution)/shard_map/ffn_bwd/pallas_call | solution.py:551
  175.1 8.4 %attn_out_bwd.1 = (f32[1024,768]{1,0:T(8,128)}, bf16[1024,768]{1,0:T(8,128)(2,1)}, bf16[2,192,768]{2,1,0:T(8,128)(2,1)}, bf16[2,192,768]{2,1,0:T(8,128)(2,1)}) custom-call(s32[3]{0:T(128)} %copy-done.23, f32[1024,768]{1,0:T(8,128)} %get-tuple-element.79.gn_ref, f32[1024,768]{1,0:T(8,128)} %get-tuple-element.80.x2_ref, f32[1,768]{1,0:T(1,128)} %reshape.290.gain_ref, ...), custom_call_target="tpu_custom_call" | custom-call | flops 3000000000 | bytes 10000000 | tf_op jit(solution)/shard_map/attn_out_bwd/pallas_call | solution.py:596
  192.4 10.6 %attn_bwd.3 = (bf16[1024,768]{1,0:T(8,128)(2,1)S(1)}, bf16[2,192,768]{2,1,0:T(8,128)(2,1)S(1)}, bf16[2,192,768]{2,1,0:T(8,128)(2,1)S(1)}, f32[2,2,8,1024]{3,2,1,0:T(8,128)S(1)}) custom-call(s32[3]{0:T(128)S(1)} %copy-done.25, bf16[1024,2304]{1,0:T(8,128)(2,1)} %copy-done.41, bf16[1024,768]{1,0:T(8,128)(2,1)S(1)} %copy-done.28, ...), custom_call_target="tpu_custom_call" | custom-call | flops 8000000000 | bytes 6000000 | tf_op jit(solution)/shard_map/attn_bwd/pallas_call | solution.py:313
  206.4 10.4 %attn_bwd.4 = (bf16[1024,768]{1,0:T(8,128)(2,1)S(1)}, bf16[2,192,768]{2,1,0:T(8,128)(2,1)S(1)}, bf16[2,192,768]{2,1,0:T(8,128)(2,1)S(1)}, f32[2,2,8,1024]{3,2,1,0:T(8,128)S(1)}) custom-call(s32[3]{0:T(128)S(1)} %copy-done.25, bf16[1024,2304]{1,0:T(8,128)(2,1)} %copy-done.41, bf16[1024,768]{1,0:T(8,128)(2,1)S(1)} %copy-done.28, ...), custom_call_target="tpu_custom_call" | custom-call | flops 8000000000 | bytes 6000000 | tf_op jit(solution)/shard_map/attn_bwd/pallas_call | solution.py:313
  218.3 10.2 %attn_bwd.5 = (bf16[1024,768]{1,0:T(8,128)(2,1)S(1)}, bf16[2,192,768]{2,1,0:T(8,128)(2,1)S(1)}, bf16[2,192,768]{2,1,0:T(8,128)(2,1)S(1)}, f32[2,2,8,1024]{3,2,1,0:T(8,128)S(1)}) custom-call(s32[3]{0:T(128)S(1)} %copy-done.25, bf16[1024,2304]{1,0:T(8,128)(2,1)} %copy-done.41, bf16[1024,768]{1,0:T(8,128)(2,1)S(1)} %copy-done.28, ...), custom_call_target="tpu_custom_call" | custom-call | flops 8000000000 | bytes 6000000 | tf_op jit(solution)/shard_map/attn_bwd/pallas_call | solution.py:313
  243.1 8.4 %collective-permute-done.40 = bf16[96,3072]{1,0:T(8,128)(2,1)} collective-permute-done((bf16[96,3072]{1,0:T(8,128)(2,1)}, bf16[96,3072]{1,0:T(8,128)(2,1)}, u32[]{:S(2)}, u32[]{:S(2)}) %collective-permute-start.40) | collective-permute-done | bytes 589856 | tf_op jit(solution)/shard_map/ppermute | solution.py:645
  255.3 11.0 %token_grad.1 = bf16[1024,768]{1,0:T(8,128)(2,1)} custom-call(s32[3]{0:T(128)} %copy-done.23, f32[1024,768]{1,0:T(8,128)} %get-tuple-element.84.gx_ref, bf16[1024,768]{1,0:T(8,128)(2,1)} %bitcast.68, f32[1,768]{1,0:T(1,128)} %copy-done.26, bf16[1024,768]{1,0:T(8,128)(2,1)} %copy-done.38, bf16[1024,768]{1,0:T(8,128)(2,1)} %copy-done.39, ...), custom_call_target="tpu_custom_call" | custom-call | flops 4000000000 | bytes 10000000 | tf_op jit(solution)/shard_map/token_grad/pallas_call | solution.py:628
  273.1 4.0 %collective-permute-done.42 = bf16[96,768]{1,0:T(8,128)(2,1)S(1)} collective-permute-done((bf16[96,768]{1,0:T(8,128)(2,1)S(1)}, bf16[96,768]{1,0:T(8,128)(2,1)S(1)}, u32[]{:S(2)}, u32[]{:S(2)}) %collective-permute-start.42) | collective-permute-done | bytes 147488 | tf_op jit(solution)/shard_map/ppermute | solution.py:645
  280.3 4.5 %collective-permute-done.43 = bf16[96,768]{1,0:T(8,128)(2,1)S(1)} collective-permute-done((bf16[96,768]{1,0:T(8,128)(2,1)S(1)}, bf16[96,768]{1,0:T(8,128)(2,1)S(1)}, u32[]{:S(2)}, u32[]{:S(2)}) %collective-permute-start.43) | collective-permute-done | bytes 147488 | tf_op jit(solution)/shard_map/ppermute | solution.py:645
  284.8 4.6 %collective-permute-start.44 = (bf16[96,1536]{1,0:T(8,128)(2,1)S(1)}, bf16[96,1536]{1,0:T(8,128)(2,1)}, u32[]{:S(2)}, u32[]{:S(2)}) collective-permute-start(bf16[96,1536]{1,0:T(8,128)(2,1)S(1)} %pad_maximum_fusion.3), channel_id=1, source_target_pairs={{0,4},{4,0},{8,12},{12,8},{1,5},{5,1},{9,13},{13,9},{2,6},{6,2},{1... | collective-permute-start | bytes 884744 | tf_op jit(solution)/shard_map/ppermute | solution.py:645
  291.0 3.3 collective-permute-done.44
  298.7 10.9 %collective-permute-done.29 = bf16[96,2304]{1,0:T(8,128)(2,1)S(1)} collective-permute-done((bf16[96,2304]{1,0:T(8,128)(2,1)S(1)}, bf16[96,2304]{1,0:T(8,128)(2,1)S(1)}, u32[]{:S(2)}, u32[]{:S(2)}) %collective-permute-start.29) | collective-permute-done | bytes 442400 | tf_op jit(solution)/shard_map/ppermute | solution.py:645
  312.7 4.8 %collective-permute-done.45 = bf16[96,3072]{1,0:T(8,128)(2,1)S(1)} collective-permute-done((bf16[96,3072]{1,0:T(8,128)(2,1)S(1)}, bf16[96,3072]{1,0:T(8,128)(2,1)S(1)}, u32[]{:S(2)}, u32[]{:S(2)}) %collective-permute-start.45) | collective-permute-done | bytes 589856 | tf_op jit(solution)/shard_map/ppermute | solution.py:645
  319.2 3.7 %collective-permute-start.31 = (bf16[96,2304]{1,0:T(8,128)(2,1)S(1)}, bf16[96,2304]{1,0:T(8,128)(2,1)S(1)}, u32[]{:S(2)}, u32[]{:S(2)}) collective-permute-start(bf16[96,2304]{1,0:T(8,128)(2,1)S(1)} %add_convert_fusion.4), channel_id=1, source_target_pairs={{0,8},{4,12},{8,0},{12,4},{1,9},{5,13},{9,1},{13,5},{2,10},{6,14},... | collective-permute-start | bytes 1327112 | tf_op jit(solution)/shard_map/ppermute | solution.py:645
  325.3 13.9 %collective-permute-done.31 = bf16[96,2304]{1,0:T(8,128)(2,1)S(1)} collective-permute-done((bf16[96,2304]{1,0:T(8,128)(2,1)S(1)}, bf16[96,2304]{1,0:T(8,128)(2,1)S(1)}, u32[]{:S(2)}, u32[]{:S(2)}) %collective-permute-start.31) | collective-permute-done | bytes 442400 | tf_op jit(solution)/shard_map/ppermute | solution.py:645
  344.5 4.9 %collective-permute-done.32 = bf16[96,2304]{1,0:T(8,128)(2,1)S(1)} collective-permute-done((bf16[96,2304]{1,0:T(8,128)(2,1)S(1)}, bf16[96,2304]{1,0:T(8,128)(2,1)S(1)}, u32[]{:S(2)}, u32[]{:S(2)}) %collective-permute-start.32) | collective-permute-done | bytes 442400 | tf_op jit(solution)/shard_map/ppermute | solution.py:645
  352.6 2.7 reshape.292
  355.3 4.7 %slice_reduce_fusion = (f32[192,6,128]{2,1,0:T(8,128)S(1)}, f32[192,6,128]{2,1,0:T(8,128)S(1)}, f32[192,6,128]{2,1,0:T(8,128)S(1)}) fusion(f32[192,6,3,128]{3,2,1,0:T(4,128)S(1)} %reshape.292), kind=kLoop, calls=%fused_computation.50 | loop fusion | bytes 3538944 | tf_op jit(solution)/shard_map/slice | solution.py:917
  (366 shorter events, 130.5 us)
Async XLA Ops:
  7.2 332.8 %all-gather.2.cloned.1.call-start = ((), (), s32[]{:S(2)}) async-start(), calls=%async_computation | async-start | bytes 3244032 | tf_op jit(solution)/shard_map/all_gather | solution.py:868
  9.5 15.8 %collective-permute-start = (bf16[1,512]{1,0:T(2,128)(2,1)S(1)}, bf16[1,512]{1,0:T(2,128)(2,1)S(1)}, u32[]{:S(2)}, u32[]{:S(2)}) collective-permute-start(bf16[1,512]{1,0:T(2,128)(2,1)S(1)} %pad_maximum_fusion.7), channel_id=1, source_target_pairs={{0,1},{1,0},{2,3},{3,2},{4,5},{5,4},{6,7},{7,6},{8,9},{9,8},{10,11... | collective-permute-start | bytes 3080 | tf_op jit(solution)/shard_map/ppermute | solution.py:645
  14.7 37.0 %collective-permute-start.2 = (bf16[192,2304]{1,0:T(8,128)(2,1)S(1)}, bf16[192,2304]{1,0:T(8,128)(2,1)}, u32[]{:S(2)}, u32[]{:S(2)}) collective-permute-start(bf16[192,2304]{1,0:T(8,128)(2,1)S(1)} %get-tuple-element.63.rest_0_.rest_3_), channel_id=1, source_target_pairs={{0,1},{1,0},{2,3},{3,2},{4,5},{5,4},{6,7},{7,6},{8,9},{9,8},{10,11... | collective-permute-start | bytes 2654216 | tf_op jit(solution)/shard_map/ppermute | solution.py:645
  14.7 15.5 %collective-permute-start.3 = (bf16[96,2304]{1,0:T(8,128)(2,1)}, bf16[96,2304]{1,0:T(8,128)(2,1)S(1)}, u32[]{:S(2)}, u32[]{:S(2)}) collective-permute-start(bf16[96,2304]{1,0:T(8,128)(2,1)} %get-tuple-element.64), channel_id=1, source_target_pairs={{0,2},{1,3},{2,0},{3,1},{4,6},{5,7},{6,4},{7,5},{8,10},{9,11},{10,... | collective-permute-start | bytes 1327112 | tf_op jit(solution)/shard_map/ppermute | solution.py:645
  20.9 77.2 %collective-permute-start.7 = (bf16[192,3840]{1,0:T(8,128)(2,1)S(1)}, bf16[192,3840]{1,0:T(8,128)(2,1)}, u32[]{:S(2)}, u32[]{:S(2)}) collective-permute-start(bf16[192,3840]{1,0:T(8,128)(2,1)S(1)} %get-tuple-element.68.rest_3_.rest_0_), channel_id=1, source_target_pairs={{0,1},{1,0},{2,3},{3,2},{4,5},{5,4},{6,7},{7,6},{8,9},{9,8},{10,11... | collective-permute-start | bytes 4423688 | tf_op jit(solution)/shard_map/ppermute | solution.py:645
  30.3 12.5 %collective-permute-start.4 = (bf16[96,2304]{1,0:T(8,128)(2,1)S(1)}, bf16[96,2304]{1,0:T(8,128)(2,1)}, u32[]{:S(2)}, u32[]{:S(2)}) collective-permute-start(bf16[96,2304]{1,0:T(8,128)(2,1)S(1)} %collective-permute-done.3.rest_2_.refs_1_.rest_5_), channel_id=1, source_target_pairs={{0,16},{16,0},{1,17},{17,1},{2,18},{18,2},{3,19},{19,3},{4,20},{20... | collective-permute-start | bytes 1327112 | tf_op jit(solution)/shard_map/ppermute | solution.py:645
  33.1 18.5 %collective-permute-start.8 = (bf16[96,3840]{1,0:T(8,128)(2,1)}, bf16[96,3840]{1,0:T(8,128)(2,1)}, u32[]{:S(2)}, u32[]{:S(2)}) collective-permute-start(bf16[96,3840]{1,0:T(8,128)(2,1)} %after.3), channel_id=1, source_target_pairs={{0,2},{1,3},{2,0},{3,1},{4,6},{5,7},{6,4},{7,5},{8,10},{9,11},{10,... | collective-permute-start | bytes 2211848 | tf_op jit(solution)/shard_map/ppermute | solution.py:645
  40.3 12.9 %collective-permute-start.5 = (bf16[96,2304]{1,0:T(8,128)(2,1)S(1)}, bf16[96,2304]{1,0:T(8,128)(2,1)}, u32[]{:S(2)}, u32[]{:S(2)}) collective-permute-start(bf16[96,2304]{1,0:T(8,128)(2,1)S(1)} %copy-done.20), channel_id=1, source_target_pairs={{0,1},{1,0},{2,3},{3,2},{4,5},{5,4},{6,7},{7,6},{8,9},{9,8},{10,11... | collective-permute-start | bytes 1327112 | tf_op jit(solution)/shard_map/ppermute | solution.py:645
  42.7 10.9 %collective-permute-start.6 = (bf16[96,2304]{1,0:T(8,128)(2,1)}, bf16[96,2304]{1,0:T(8,128)(2,1)S(1)}, u32[]{:S(2)}, u32[]{:S(2)}) collective-permute-start(bf16[96,2304]{1,0:T(8,128)(2,1)} %collective-permute-done.4.rest_3_.rest_6_), channel_id=1, source_target_pairs={{0,1},{1,0},{2,3},{3,2},{4,5},{5,4},{6,7},{7,6},{8,9},{9,8},{10,11... | collective-permute-start | bytes 1327112 | tf_op jit(solution)/shard_map/ppermute | solution.py:645
  51.6 66.4 %collective-permute-start.12 = (bf16[960,768]{1,0:T(8,128)(2,1)}, bf16[960,768]{1,0:T(8,128)(2,1)}, u32[]{:S(2)}, u32[]{:S(2)}) collective-permute-start(bf16[960,768]{1,0:T(8,128)(2,1)} %copy-done.29), channel_id=1, source_target_pairs={{0,1},{1,0},{2,3},{3,2},{4,5},{5,4},{6,7},{7,6},{8,9},{9,8},{10,11... | collective-permute-start | bytes 4423688 | tf_op jit(solution)/shard_map/ppermute | solution.py:645
  51.6 23.7 %collective-permute-start.13 = (bf16[480,768]{1,0:T(8,128)(2,1)}, bf16[480,768]{1,0:T(8,128)(2,1)S(1)}, u32[]{:S(2)}, u32[]{:S(2)}) collective-permute-start(bf16[480,768]{1,0:T(8,128)(2,1)} %after.4), channel_id=1, source_target_pairs={{0,2},{1,3},{2,0},{3,1},{4,6},{5,7},{6,4},{7,5},{8,10},{9,11},{10,... | collective-permute-start | bytes 2211848 | tf_op jit(solution)/shard_map/ppermute | solution.py:645
  53.2 21.7 %collective-permute-start.9 = (bf16[96,3840]{1,0:T(8,128)(2,1)}, bf16[96,3840]{1,0:T(8,128)(2,1)S(1)}, u32[]{:S(2)}, u32[]{:S(2)}) collective-permute-start(bf16[96,3840]{1,0:T(8,128)(2,1)} %collective-permute-done.8.rest_5_.refs_1_.rest_2_), channel_id=1, source_target_pairs={{0,16},{16,0},{1,17},{17,1},{2,18},{18,2},{3,19},{19,3},{4,20},{20... | collective-permute-start | bytes 2211848 | tf_op jit(solution)/shard_map/ppermute | solution.py:645
  54.5 44.1 %collective-permute-start.10 = (bf16[96,3840]{1,0:T(8,128)(2,1)}, bf16[96,3840]{1,0:T(8,128)(2,1)S(1)}, u32[]{:S(2)}, u32[]{:S(2)}) collective-permute-start(bf16[96,3840]{1,0:T(8,128)(2,1)} %collective-permute-done.8.rest_5_.refs_1_.rest_2_), channel_id=1, source_target_pairs={{0,1},{1,0},{2,3},{3,2},{4,5},{5,4},{6,7},{7,6},{8,9},{9,8},{10,11... | collective-permute-start | bytes 2211848 | tf_op jit(solution)/shard_map/ppermute | solution.py:645
  74.8 23.8 %collective-permute-start.11 = (bf16[96,3840]{1,0:T(8,128)(2,1)S(1)}, bf16[96,3840]{1,0:T(8,128)(2,1)S(1)}, u32[]{:S(2)}, u32[]{:S(2)}) collective-permute-start(bf16[96,3840]{1,0:T(8,128)(2,1)S(1)} %collective-permute-done.9.rest_6_.rest_3_), channel_id=1, source_target_pairs={{0,1},{1,0},{2,3},{3,2},{4,5},{5,4},{6,7},{7,6},{8,9},{9,8},{10,11... | collective-permute-start | bytes 2211848 | tf_op jit(solution)/shard_map/ppermute | solution.py:645
  75.3 22.8 %collective-permute-start.14 = (bf16[480,768]{1,0:T(8,128)(2,1)S(1)}, bf16[480,768]{1,0:T(8,128)(2,1)S(1)}, u32[]{:S(2)}, u32[]{:S(2)}) collective-permute-start(bf16[480,768]{1,0:T(8,128)(2,1)S(1)} %collective-permute-done.13.rest_2_.rest_8_), channel_id=1, source_target_pairs={{0,16},{16,0},{1,17},{17,1},{2,18},{18,2},{3,19},{19,3},{4,20},{20... | collective-permute-start | bytes 2211848 | tf_op jit(solution)/shard_map/ppermute | solution.py:645
  98.1 19.9 %collective-permute-start.15 = (bf16[480,768]{1,0:T(8,128)(2,1)S(1)}, bf16[480,768]{1,0:T(8,128)(2,1)S(1)}, u32[]{:S(2)}, u32[]{:S(2)}) collective-permute-start(bf16[480,768]{1,0:T(8,128)(2,1)S(1)} %collective-permute-done.13.rest_2_.rest_8_), channel_id=1, source_target_pairs={{0,1},{1,0},{2,3},{3,2},{4,5},{5,4},{6,7},{7,6},{8,9},{9,8},{10,11... | collective-permute-start | bytes 2211848 | tf_op jit(solution)/shard_map/ppermute | solution.py:645
  98.1 19.9 %collective-permute-start.16 = (bf16[480,768]{1,0:T(8,128)(2,1)S(1)}, bf16[480,768]{1,0:T(8,128)(2,1)S(1)}, u32[]{:S(2)}, u32[]{:S(2)}) collective-permute-start(bf16[480,768]{1,0:T(8,128)(2,1)S(1)} %collective-permute-done.14.rest_3_.rest_9_), channel_id=1, source_target_pairs={{0,1},{1,0},{2,3},{3,2},{4,5},{5,4},{6,7},{7,6},{8,9},{9,8},{10,11... | collective-permute-start | bytes 2211848 | tf_op jit(solution)/shard_map/ppermute | solution.py:645
  174.9 11.9 %collective-permute-start.26 = (bf16[2,192,3072]{2,1,0:T(8,128)(2,1)}, bf16[2,192,3072]{2,1,0:T(8,128)(2,1)S(1)}, u32[]{:S(2)}, u32[]{:S(2)}) collective-permute-start(bf16[2,192,3072]{2,1,0:T(8,128)(2,1)} %get-tuple-element.90), channel_id=1, source_target_pairs={{0,1},{1,0},{2,3},{3,2},{4,5},{5,4},{6,7},{7,6},{8,9},{9,8},{10,11... | collective-permute-start | bytes 7077896 | tf_op jit(solution)/shard_map/ppermute | solution.py:645
  190.7 45.3 %collective-permute-start.39 = (bf16[192,3072]{1,0:T(8,128)(2,1)S(1)}, bf16[192,3072]{1,0:T(8,128)(2,1)S(1)}, u32[]{:S(2)}, u32[]{:S(2)}) collective-permute-start(bf16[192,3072]{1,0:T(8,128)(2,1)S(1)} %get-tuple-element.154.rest_0_), channel_id=1, source_target_pairs={{0,2},{1,3},{2,0},{3,1},{4,6},{5,7},{6,4},{7,5},{8,10},{9,11},{10,... | collective-permute-start | bytes 3538952 | tf_op jit(solution)/shard_map/ppermute | solution.py:645
  218.0 21.7 %collective-permute-start.27 = (bf16[2,192,2304]{2,1,0:T(8,128)(2,1)S(1)}, bf16[2,192,2304]{2,1,0:T(8,128)(2,1)S(1)}, u32[]{:S(2)}, u32[]{:S(2)}) collective-permute-start(bf16[2,192,2304]{2,1,0:T(8,128)(2,1)S(1)} %constant_dynamic-update-slice_fusion.8.rest_0_), channel_id=1, source_target_pairs={{0,1},{1,0},{2,3},{3,2},{4,5},{5,4},{6,7},{7,6},{8,9},{9,8},{10,11... | collective-permute-start | bytes 5308424 | tf_op jit(solution)/shard_map/ppermute | solution.py:645
  228.6 10.1 %collective-permute-start.33 = (bf16[2,192,768]{2,1,0:T(8,128)(2,1)S(1)}, bf16[2,192,768]{2,1,0:T(8,128)(2,1)S(1)}, u32[]{:S(2)}, u32[]{:S(2)}) collective-permute-start(bf16[2,192,768]{2,1,0:T(8,128)(2,1)S(1)} %get-tuple-element.105), channel_id=1, source_target_pairs={{0,1},{1,0},{2,3},{3,2},{4,5},{5,4},{6,7},{7,6},{8,9},{9,8},{10,11... | collective-permute-start | bytes 1769480 | tf_op jit(solution)/shard_map/ppermute | solution.py:645
  237.1 14.5 %collective-permute-start.40 = (bf16[96,3072]{1,0:T(8,128)(2,1)}, bf16[96,3072]{1,0:T(8,128)(2,1)}, u32[]{:S(2)}, u32[]{:S(2)}) collective-permute-start(bf16[96,3072]{1,0:T(8,128)(2,1)} %get-tuple-element.155), channel_id=1, source_target_pairs={{0,16},{16,0},{1,17},{17,1},{2,18},{18,2},{3,19},{19,3},{4,20},{20... | collective-permute-start | bytes 1769480 | tf_op jit(solution)/shard_map/ppermute | solution.py:645
  241.0 11.8 %collective-permute-start.34 = (bf16[192,768]{1,0:T(8,128)(2,1)}, bf16[192,768]{1,0:T(8,128)(2,1)S(1)}, u32[]{:S(2)}, u32[]{:S(2)}) collective-permute-start(bf16[192,768]{1,0:T(8,128)(2,1)} %after.5), channel_id=1, source_target_pairs={{0,2},{1,3},{2,0},{3,1},{4,6},{5,7},{6,4},{7,5},{8,10},{9,11},{10,... | collective-permute-start | bytes 884744 | tf_op jit(solution)/shard_map/ppermute | solution.py:645
  243.1 23.2 %collective-permute-start.49 = (f32[32,12]{0,1:T(8,128)S(1)}, f32[32,12]{0,1:T(8,128)S(1)}, u32[]{:S(2)}, u32[]{:S(2)}) collective-permute-start(f32[32,12]{0,1:T(8,128)S(1)} %add.381), channel_id=1, source_target_pairs={{0,4},{4,0},{8,12},{12,8},{1,5},{5,1},{9,13},{13,9},{2,6},{6,2},{1... | collective-permute-start | bytes 4616 | tf_op jit(solution)/shard_map/ppermute | solution.py:645
  252.7 16.4 %collective-permute-start.41 = (bf16[96,1536]{1,0:T(8,128)(2,1)S(1)}, bf16[96,1536]{1,0:T(8,128)(2,1)S(1)}, u32[]{:S(2)}, u32[]{:S(2)}) collective-permute-start(bf16[96,1536]{1,0:T(8,128)(2,1)S(1)} %get-tuple-element.159), channel_id=1, source_target_pairs={{0,4},{4,0},{8,12},{12,8},{1,5},{5,1},{9,13},{13,9},{2,6},{6,2},{1... | collective-permute-start | bytes 884744 | tf_op jit(solution)/shard_map/ppermute | solution.py:645
  253.8 17.1 %collective-permute-start.35 = (bf16[96,768]{1,0:T(8,128)(2,1)S(1)}, bf16[96,768]{1,0:T(8,128)(2,1)S(1)}, u32[]{:S(2)}, u32[]{:S(2)}) collective-permute-start(bf16[96,768]{1,0:T(8,128)(2,1)S(1)} %fusion.53), channel_id=1, source_target_pairs={{0,16},{16,0},{1,17},{17,1},{2,18},{18,2},{3,19},{19,3},{4,20},{20... | collective-permute-start | bytes 442376 | tf_op jit(solution)/shard_map/ppermute | solution.py:645
  266.3 23.1 %collective-permute-start.50 = (f32[32,12]{0,1:T(8,128)S(1)}, f32[32,12]{0,1:T(8,128)S(1)}, u32[]{:S(2)}, u32[]{:S(2)}) collective-permute-start(f32[32,12]{0,1:T(8,128)S(1)} %add.382), channel_id=1, source_target_pairs={{0,8},{4,12},{8,0},{12,4},{1,9},{5,13},{9,1},{13,5},{2,10},{6,14},... | collective-permute-start | bytes 4616 | tf_op jit(solution)/shard_map/ppermute | solution.py:645
  267.7 27.6 %collective-permute-start.28 = (bf16[192,2304]{1,0:T(8,128)(2,1)S(1)}, bf16[192,2304]{1,0:T(8,128)(2,1)}, u32[]{:S(2)}, u32[]{:S(2)}) collective-permute-start(bf16[192,2304]{1,0:T(8,128)(2,1)S(1)} %copy-done.61), channel_id=1, source_target_pairs={{0,2},{1,3},{2,0},{3,1},{4,6},{5,7},{6,4},{7,5},{8,10},{9,11},{10,... | collective-permute-start | bytes 2654216 | tf_op jit(solution)/shard_map/ppermute | solution.py:645
  277.7 12.5 %collective-permute-start.37 = (bf16[96,768]{1,0:T(8,128)(2,1)S(1)}, bf16[96,768]{1,0:T(8,128)(2,1)S(1)}, u32[]{:S(2)}, u32[]{:S(2)}) collective-permute-start(bf16[96,768]{1,0:T(8,128)(2,1)S(1)} %add_convert_fusion.10), channel_id=1, source_target_pairs={{0,8},{4,12},{8,0},{12,4},{1,9},{5,13},{9,1},{13,5},{2,10},{6,14},... | collective-permute-start | bytes 442376 | tf_op jit(solution)/shard_map/ppermute | solution.py:645
  296.4 13.2 %collective-permute-start.29 = (bf16[96,2304]{1,0:T(8,128)(2,1)S(1)}, bf16[96,2304]{1,0:T(8,128)(2,1)S(1)}, u32[]{:S(2)}, u32[]{:S(2)}) collective-permute-start(bf16[96,2304]{1,0:T(8,128)(2,1)S(1)} %fusion.45), channel_id=1, source_target_pairs={{0,16},{16,0},{1,17},{17,1},{2,18},{18,2},{3,19},{19,3},{4,20},{20... | collective-permute-start | bytes 1327112 | tf_op jit(solution)/shard_map/ppermute | solution.py:645
  297.2 20.4 %collective-permute-start.45 = (bf16[96,3072]{1,0:T(8,128)(2,1)S(1)}, bf16[96,3072]{1,0:T(8,128)(2,1)S(1)}, u32[]{:S(2)}, u32[]{:S(2)}) collective-permute-start(bf16[96,3072]{1,0:T(8,128)(2,1)S(1)} %pad_maximum_fusion), channel_id=1, source_target_pairs={{0,16},{16,0},{1,17},{17,1},{2,18},{18,2},{3,19},{19,3},{4,20},{20... | collective-permute-start | bytes 1769480 | tf_op jit(solution)/shard_map/ppermute | solution.py:645
  319.2 19.9 %collective-permute-start.31 = (bf16[96,2304]{1,0:T(8,128)(2,1)S(1)}, bf16[96,2304]{1,0:T(8,128)(2,1)S(1)}, u32[]{:S(2)}, u32[]{:S(2)}) collective-permute-start(bf16[96,2304]{1,0:T(8,128)(2,1)S(1)} %add_convert_fusion.4), channel_id=1, source_target_pairs={{0,8},{4,12},{8,0},{12,4},{1,9},{5,13},{9,1},{13,5},{2,10},{6,14},... | collective-permute-start | bytes 1327112 | tf_op jit(solution)/shard_map/ppermute | solution.py:645
  (97 other events, 593.8 us)
Sparse Core Ops, SparseCore 0:
  175.2 59.7 all-gather.1
